TPU v7x, 32 devices: a whole 2x2x4 slice. The times are simulated.
32 devices in a mesh: dp: 8 (over z, x), head: 4 (over y, core).
Axes of the slice: x: 2, y: 2, z: 4, core: 2. Of those that a mesh axis runs over, the one named last changes fastest.
Arguments:
- tokens: bfloat16 [8192, 768], P(('dp', 'head')), may hold values from -6 to 6
- cotangent: bfloat16 [8192, 768], P(('dp', 'head')), may hold values from -6 to 6
- qkv_weight: bfloat16 [768, 2304], replicated, may hold values from -0.21875 to 0.21875
- out_weight: bfloat16 [768, 768], replicated, may hold values from -0.875 to 0.875
- up_weight: bfloat16 [768, 3072], replicated, may hold values from -0.21875 to 0.21875
- down_weight: bfloat16 [3072, 768], replicated, may hold values from -0.109375 to 0.109375
- vectors: float32 [9216], replicated, may hold values from -1.2 to 1.4
- qkv_moment: float32 [768, 2304], P(None, 'dp'), may hold values from -160 to 160
- out_moment: float32 [768, 768], P(None, 'dp'), may hold values from -160 to 160
- up_moment: float32 [768, 3072], P(None, 'dp'), may hold values from -128 to 128
- down_moment: float32 [768, 3072], P(None, 'dp'), may hold values from -256 to 256
- adam_first: float32 [9216], P('dp'), may hold values from -120.67956 to 120.67956
- adam_second: float32 [9216], P('dp'), may hold values from 2.05005 to 295.2072
- bucket_class: int32 [8], P('dp'), may hold values from 0 to 2, as said below
- row_lengths: int32 [8, 8], P('dp'), may hold values from 0 to 512, as said below
Outputs:
- mixed: float32 [8192, 768], P(('dp', 'head'))
- input_grad: float32 [8192, 768], P(('dp', 'head'))
- qkv_moment_new: float32 [768, 2304], P(None, 'dp')
- out_moment_new: float32 [768, 768], P(None, 'dp')
- up_moment_new: float32 [768, 3072], P(None, 'dp')
- down_moment_new: float32 [768, 3072], P(None, 'dp')
- new_qkv: float32 [768, 2304], P(None, 'dp')
- new_out: float32 [768, 768], P(None, 'dp')
- new_up: float32 [768, 3072], P(None, 'dp')
- new_down: float32 [3072, 768], P('dp')
- vector_moment: float32 [9216], P('dp')
- vector_second: float32 [9216], P('dp')
- vector_new: float32 [9216], P('dp')
Inputs may be any that keep to these rules, and one draw needn't show every extreme that they name: `bucket_class`: every class 0, 1, 2 occurs. `row_lengths`: with span = 128 * 2 ** bucket_class[g], entries 0 to 1024 / span - 1 of bucket g are lengths from 1 to span, one of them equal to span; the other entries are 0.
All inputs are finite; a program needn't handle non-finite values.
Results may differ from a plain program's by a relative error of at most 0.019.
Values may be sent and summed in bfloat16 or wider, within the bound.
A program may use at most 256 MiB of HBM per device.

v0:
```python
import functools
import itertools
import math

import jax
import jax.numpy as jnp
from jax import lax
from jax.experimental import pallas as pl
from jax.experimental.pallas import tpu as pltpu
from jax.sharding import PartitionSpec as P

D = 768
HEADS = 12
HEAD_DIM = 64
FF = 3072
BASE_LEN = 128
NS_STEPS = 5
STEP = 5
MAX_LEN = 512

f32 = jnp.float32
bf16 = jnp.bfloat16

norm_eps = 1e-12
masked_score = -1000000000.0
quintic_a = 3.4445
quintic_b = -4.775
quintic_c = 2.0315
muon_rate = 1.0
muon_decay = 0.01
muon_keep = 0.5
adam_rate = 0.2
beta_first = 0.9
beta_second = 0.999
adam_eps = 1e-08
MIB = 1024 * 1024


def dot(left, right, left_dim, right_dim):
    return lax.dot_general(
        left, right, (((left_dim,), (right_dim,)), ((), ())), preferred_element_type=f32
    )


def split_vectors(vectors, width, hidden):
    lengths_list = [width] * 5 + [hidden] + [width] * 3
    pieces = []
    offset = 0
    for length in lengths_list:
        pieces.append(vectors[offset : offset + length])
        offset = offset + length
    return pieces


def allowed_mask(class_ref, length_ref, block, tok):
    shift = class_ref[0] + int(math.log2(BASE_LEN))
    query_place = block * tok + lax.broadcasted_iota(jnp.int32, (tok, 1), 0)
    lane = lax.broadcasted_iota(jnp.int32, (1, 2 * tok), 1)
    own = lane < tok
    key_place = jnp.where(own, block * tok + lane, (block ^ 1) * tok + lane - tok)
    key_row = lax.shift_right_logical(key_place, jnp.broadcast_to(shift, key_place.shape))
    offset = key_place - lax.shift_left(key_row, jnp.broadcast_to(shift, key_place.shape))
    row_len = jnp.zeros_like(key_row)
    for slot in range(length_ref.shape[1]):
        row_len = jnp.where(key_row == slot, length_ref[0, slot], row_len)
    key_row = jnp.where(offset < row_len, key_row, -1)
    query_row = lax.shift_right_logical(query_place, jnp.broadcast_to(shift, query_place.shape))
    return query_row == key_row


def half_masks():
    lane = lax.broadcasted_iota(jnp.int32, (1, 2 * HEAD_DIM), 1)
    first = (lane < HEAD_DIM).astype(f32)
    return (first.astype(bf16), (1.0 - first).astype(bf16)), lane < HEAD_DIM


def head_prob(query, keys, allowed):
    score = jnp.where(allowed, dot(query, keys, 1, 1) * HEAD_DIM ** (-0.5), masked_score)
    exponent = jnp.exp(score - jnp.max(score, axis=-1, keepdims=True))
    return exponent / jnp.sum(exponent, axis=-1, keepdims=True)


def attend_kernel(block_ref, class_ref, length_ref, qkv_ref, other_ref, out_ref):
    tok = qkv_ref.shape[0]
    allowed = allowed_mask(class_ref, length_ref, block_ref[0], tok)
    masks, first = half_masks()
    for pair in range(HEADS // 2):
        cols = pl.ds(pair * 2 * HEAD_DIM, 2 * HEAD_DIM)
        kcols = pl.ds(D + pair * 2 * HEAD_DIM, 2 * HEAD_DIM)
        vcols = pl.ds(2 * D + pair * 2 * HEAD_DIM, 2 * HEAD_DIM)
        query = qkv_ref[:, cols]
        keys = jnp.concatenate([qkv_ref[:, kcols], other_ref[:, cols]], axis=0)
        values = jnp.concatenate([qkv_ref[:, vcols], other_ref[:, kcols]], axis=0)
        outs = []
        for mask in masks:
            prob = head_prob(query * mask, keys, allowed)
            outs.append(dot(prob.astype(bf16), values, 1, 0))
        out_ref[:, cols] = jnp.where(first, outs[0], outs[1]).astype(bf16)


def attend_back_kernel(
    block_ref, class_ref, length_ref, qkv_ref, other_ref, grad_ref, dq_ref, own_ref, send_ref
):
    tok = qkv_ref.shape[0]
    allowed = allowed_mask(class_ref, length_ref, block_ref[0], tok)
    masks, first = half_masks()
    scale = HEAD_DIM ** (-0.5)
    for pair in range(HEADS // 2):
        cols = pl.ds(pair * 2 * HEAD_DIM, 2 * HEAD_DIM)
        kcols = pl.ds(D + pair * 2 * HEAD_DIM, 2 * HEAD_DIM)
        vcols = pl.ds(2 * D + pair * 2 * HEAD_DIM, 2 * HEAD_DIM)
        query = qkv_ref[:, cols]
        keys = jnp.concatenate([qkv_ref[:, kcols], other_ref[:, cols]], axis=0)
        values = jnp.concatenate([qkv_ref[:, vcols], other_ref[:, kcols]], axis=0)
        grad = grad_ref[:, cols]
        dqs, dk, dv = [], None, None
        for mask in masks:
            head_query = query * mask
            head_grad = grad * mask
            prob = head_prob(head_query, keys, allowed)
            part_v = dot(prob.astype(bf16), head_grad, 0, 0)
            dprob = dot(head_grad, values, 1, 1)
            dscore = prob * (dprob - jnp.sum(prob * dprob, axis=-1, keepdims=True))
            dscore = dscore.astype(bf16)
            dqs.append(dot(dscore, keys, 1, 0))
            part_k = dot(dscore, head_query, 0, 0)
            dk = part_k if dk is None else dk + part_k
            dv = part_v if dv is None else dv + part_v
        dk = dk * scale
        dq_ref[:, cols] = (jnp.where(first, dqs[0], dqs[1]) * scale).astype(bf16)
        own_ref[:, cols] = dk[:tok]
        own_ref[:, kcols] = dv[:tok]
        send_ref[:, cols] = dk[tok:].astype(bf16)
        send_ref[:, kcols] = dv[tok:].astype(bf16)


SMEM = pl.BlockSpec(memory_space=pltpu.SMEM)
VMEM = pl.BlockSpec(memory_space=pltpu.VMEM)
ANY = pl.BlockSpec(memory_space=pl.ANY)


def attend(block, row_class, lengths, qkv, other):
    tok = qkv.shape[0]
    return pl.pallas_call(
        attend_kernel,
        out_shape=jax.ShapeDtypeStruct((tok, D), bf16),
        in_specs=[SMEM, SMEM, SMEM, VMEM, VMEM],
        out_specs=VMEM,
        compiler_params=pltpu.CompilerParams(vmem_limit_bytes=32 * MIB),
        name="attend",
    )(block, row_class, lengths, qkv, other)


def attend_back(block, row_class, lengths, qkv, other, grad):
    tok = qkv.shape[0]
    return pl.pallas_call(
        attend_back_kernel,
        out_shape=(
            jax.ShapeDtypeStruct((tok, D), bf16),
            jax.ShapeDtypeStruct((tok, 2 * D), f32),
            jax.ShapeDtypeStruct((tok, 2 * D), bf16),
        ),
        in_specs=[SMEM, SMEM, SMEM, VMEM, VMEM, VMEM],
        out_specs=(VMEM, VMEM, VMEM),
        compiler_params=pltpu.CompilerParams(vmem_limit_bytes=32 * MIB),
        name="attend_back",
    )(block, row_class, lengths, qkv, other, grad)


CENTRES = (0.0, 0.0, 0.0, 0.8, 0.8)
TILE = 256
SUB = 128


def sub_blocks(size):
    count = size // SUB
    return [(i, j) for i in range(count) for j in range(i, count)]


def newton_schulz(gram, moment, e, f, g, eb, fb, gb, yy, y, emit):
    size = e.shape[0]
    tiles = [slice(i * TILE, (i + 1) * TILE) for i in range(size // TILE)]

    def unit(rows):
        row_id = rows.start + lax.broadcasted_iota(jnp.int32, (TILE, size), 0)
        col_id = lax.broadcasted_iota(jnp.int32, (TILE, size), 1)
        return (row_id == col_id).astype(f32)

    diagonal = jnp.zeros((TILE, size), f32)
    for rows in tiles:
        diagonal = diagonal + gram[rows, :] * unit(rows)
    trace = jnp.sum(jnp.sum(diagonal, axis=0, keepdims=True), axis=1, keepdims=True)
    factor = 1.0 / (jnp.sqrt(trace) + 1e-07)
    square_factor = factor * factor
    for rows in tiles:
        value = gram[rows, :] * square_factor
        e[rows, :] = value
        eb[rows, :] = value.astype(bf16)
        value = moment[rows, :] * factor
        y[rows, :] = value
        yy[0, rows, :] = value.astype(bf16)

    def one_step(centre, after, now, then, last=False):
        keep = quintic_a + quintic_b * centre + quintic_c * centre * centre
        linear = quintic_b + 2.0 * quintic_c * centre
        for rows in tiles:
            value = linear * e[rows, :] + quintic_c * dot(eb[rows, :], eb[...], 1, 0)
            fb[rows, :] = value.astype(bf16)
            if centre:
                f[rows, :] = value
        for rows in tiles:
            value = keep * y[rows, :] + dot(fb[rows, :], now[...], 1, 0)
            if last:
                emit(rows, value.astype(bf16))
            else:
                y[rows, :] = value
                then[rows, :] = value.astype(bf16)
        if last:
            return
        for rows in tiles:
            value = keep * e[rows, :] + dot(eb[rows, :], fb[...], 1, 0)
            if centre:
                value = value + centre * f[rows, :]
            g[rows, :] = value
            gb[rows, :] = value.astype(bf16)
        for rows in tiles:
            value = keep * g[rows, :] + dot(gb[rows, :], fb[...], 1, 0)
            if centre:
                value = value + (centre * keep) * f[rows, :]
            shift = centre * keep * keep - after
            if not isinstance(shift, float) or shift:
                value = value + shift * unit(rows)
            e[rows, :] = value
            eb[rows, :] = value.astype(bf16)

    plain = sum(centre == 0.0 for centre in CENTRES)

    def plain_step(step, carry):
        after = jnp.where(step == plain - 1, CENTRES[plain], 0.0)
        one_step(0.0, after, yy.at[step % 2], yy.at[(step + 1) % 2])
        return carry

    lax.fori_loop(0, plain, plain_step, 0)
    for step in range(plain, NS_STEPS):
        last = step + 1 == NS_STEPS
        after = 0.0 if last else CENTRES[step + 1]
        one_step(CENTRES[step], after, yy.at[step % 2], yy.at[(step + 1) % 2], last)


def ortho_kernel(gram, moment, out, *scratch):
    def emit(rows, value):
        out[rows, :] = value

    newton_schulz(gram, moment, *scratch, emit)


def ortho_scratch(size, cols):
    square, square_low = pltpu.VMEM((size, size), f32), pltpu.VMEM((size, size), bf16)
    wide_low = pltpu.VMEM((2, size, cols), bf16)
    return [square] * 3 + [square_low] * 3 + [wide_low, pltpu.VMEM((size, cols), f32)]


def orthogonalize(gram_mat, moment):
    size, cols = moment.shape
    return pl.pallas_call(
        ortho_kernel,
        out_shape=jax.ShapeDtypeStruct((size, cols), bf16),
        in_specs=[VMEM, VMEM],
        out_specs=VMEM,
        scratch_shapes=ortho_scratch(size, cols),
        compiler_params=pltpu.CompilerParams(vmem_limit_bytes=48 * MIB),
        name="ortho",
    )(gram_mat, moment)


MESH = pl.DeviceIdType.MESH
PIECE = 48
SIDE = 192
UNIT = 2 * SIDE
HALF = D // 2
LANES = 128
VEC_BLOCK = 9
ROWS = 16
CHUNKS = (
    (0, 0, 64, "nfyx"),
    (0, 64, 64, "xynf"),
    (0, 128, 64, "yxnf"),
    (1, 0, 64, "ynxf"),
    (1, 64, 64, "nxyf"),
    (1, 128, 64, "xynf"),
    (2, 0, 48, "xynf"),
    (2, 48, 48, "nxyf"),
    (2, 96, 48, "yxnf"),
    (2, 144, 32, "xynf"),
    (2, 176, 16, "xfyn"),
)
CHUNK_PLAN = (
    (0, 1, 2),
    (),
    (),
    (),
    (),
    (3, 5, 4),
    (0, 1, 2),
    (),
    (),
    (),
    (0, 1, 2, 4, 5, 3),
    (),
    (),
    (0, 7, 8, 10, 9, 6),
    (
        1, 4, 2, 5, 0, 1, 10, 4, 0, 2, 0, 1, 9, 1, 3, 2, 5, 10, 4, 8, 2, 6,
        10, 5, 9, 3, 4, 10, 7, 4, 8, 10, 5, 9, 3, 10, 5, 6, 9, 8, 7, 3, 9, 6,
        3, 9, 8, 7, 8, 6, 8, 7, 6, 7, 6, 7,
    ),
)
BIAS_QUERY, BIAS_VALUE, BIAS_OUT, GAIN_ONE, SHIFT_ONE, BIAS_UP = (i * D for i in range(6))
BIAS_DOWN, GAIN_TWO, SHIFT_TWO = (BIAS_UP + FF + i * D for i in range(3))


def position():
    dp_id, head_id = lax.axis_index("dp"), lax.axis_index("head")
    z, x = dp_id // 2, dp_id % 2
    y, core = head_id // 2, head_id % 2
    return z, x, y, core


def device(z, x, y, core):
    return (2 * z + x, 2 * y + core)


def flip_z(z, step):
    high, low = z // 2, z % 2
    high = 1 - high if step // 2 else high
    low = 1 - low if step % 2 else low
    return 2 * high + low


def greet(others):
    barrier = pltpu.get_barrier_semaphore()
    for other in others:
        pl.semaphore_signal(barrier, inc=1, device_id=other, device_id_type=MESH)
    return lambda: pl.semaphore_wait(barrier, len(others))


def by_rows(count, body, init=None, together=4):
    def step(index, carry):
        for part in range(together):
            start = (index * together + part) * ROWS
            carry = body(pl.ds(pl.multiple_of(start, ROWS), ROWS), carry)
        return carry

    return lax.fori_loop(0, count // (ROWS * together), step, init)


def row_mean(value):
    return jnp.sum(value, axis=-1, keepdims=True) * (1.0 / D)


def fold(value):
    return jnp.sum(value.reshape(value.shape[0] // 8, 8, value.shape[1]), axis=0)


def column_sum(value):
    return jnp.sum(value, axis=0, keepdims=True)


def normal_parts(value):
    size = jnp.abs(value)
    decay = jnp.exp(-0.5 * value * value)
    below = 1.0 + (0.3275911 * 0.5**0.5) * size
    t = pl.reciprocal(below, approx=True)
    t = t * (2.0 - below * t)
    series = t * (1.061405429 * 0.5)
    for term in (-1.453152027, 1.421413741, -0.284496736, 0.254829592):
        series = (series + term * 0.5) * t
    tail = series * decay
    return jnp.where(value < 0.0, tail, 1.0 - tail), decay * (1.0 / math.sqrt(2.0 * math.pi))


def transposed(value):
    side = 2 * LANES
    row_id = lax.broadcasted_iota(jnp.int32, (side, side), 0)
    unit = (row_id == lax.broadcasted_iota(jnp.int32, (side, side), 1)).astype(f32).astype(bf16)
    blocks = []
    for start in range(0, value.shape[1], side):
        block = value[:, start : start + side]
        size = block.shape[1]
        blocks.append(dot(unit[:size, :size], block, 1, 1).astype(bf16))
    return jnp.concatenate(blocks, axis=0)


def layer_kernel(
    row_class,
    lengths,
    tokens,
    cotangent,
    vectors,
    qkv_hbm,
    out_hbm,
    up_hbm,
    down_hbm,
    mixed,
    input_grad,
    sums,
    vec_sum,
    qkv_w,
    out_w,
    up_w,
    down_w,
    query,
    query_turned,
    keys_values,
    keys_turned,
    prob,
    attended,
    normed_low,
    grad_down,
    grad_attn,
    narrow_tokens,
    narrow_attended,
    narrow_normed,
    narrow_grad,
    active,
    grad_up,
    attn_turned,
    qkv_turned,
    exchanged,
    grad_heads,
    heads_turned,
    slope,
    normed_one,
    zhat_one,
    rstd_one,
    grad_two,
    work,
    vec,
    vec_core,
    vec_y,
    vec_x,
    vec_z,
    part,
    came_one,
    came_two,
    came_three,
    came_four,
    load_sem,
    pair_send,
    pair_recv,
    send_sem,
    recv_sem,
):
    grad_one = normed_one
    z, x, y, core = position()
    tok = tokens.shape[0]
    loads = {
        name: pltpu.make_async_copy(source, target, load_sem.at[index])
        for index, (name, source, target) in enumerate(
            (
                ("qkv", qkv_hbm, qkv_w),
                ("out", out_hbm, out_w),
                ("up", up_hbm, up_w),
                ("down", down_hbm, down_w),
            )
        )
    }
    loads["qkv"].start()
    beyond = device(z, x, 1 - y, core)
    beside = device(z, 1 - x, y, core)
    partner = device(z, x, y, 1 - core)
    along = [device(flip_z(z, step), x, y, core) for step in (1, 2, 3)]
    all_here = greet([beyond, beside, partner] + along)
    started = []

    def remote(source, target, send_at, recv_at, other):
        copy = pltpu.make_async_remote_copy(
            src_ref=source,
            dst_ref=target,
            send_sem=send_at,
            recv_sem=recv_at,
            device_id=other,
            device_id_type=MESH,
        )
        copy.start()
        started.append(copy)
        return copy

    pair_count = []

    def to_partner(source, target):
        slot = len(pair_count)
        pair_count.append(slot)
        return remote(source, target, pair_send.at[slot], pair_recv.at[slot], partner)

    own_half = pl.ds(pl.multiple_of(core * HALF, HALF), HALF)
    other_half = pl.ds(pl.multiple_of((1 - core) * HALF, HALF), HALF)

    def span(start, length=D):
        return vectors[0:1, start : start + length]

    def put_vec(start, value):
        for index in range(value.shape[1] // LANES):
            block, row = divmod(start // LANES + index, VEC_BLOCK)
            vec[block, row : row + 1, :] = value[:, index * LANES : (index + 1) * LANES]

    vec[...] = jnp.zeros_like(vec)

    own_rows = pl.ds(0, tok)
    far_rows = pl.ds(tok, tok)
    own_lanes, far_lanes = own_rows, far_rows

    def share_half(value, narrow):
        narrow[own_rows, :] = value[:, own_half]
        return to_partner(value.at[:, other_half], narrow.at[far_rows])

    loads["qkv"].wait()
    for name in ("out", "up", "down"):
        loads[name].start()
    kv_came = []
    for index, start in ((1, None), (2, BIAS_VALUE)):
        value = dot(tokens[...], qkv_w[:, index * D : (index + 1) * D], 1, 0)
        if start is not None:
            value = value + span(start)
        cols = slice((index - 1) * D, index * D)
        keys_values[own_rows, cols] = value.astype(bf16)
        if index == 1:
            all_here()
        kv_came.append(
            to_partner(keys_values.at[own_rows, cols], keys_values.at[far_rows, cols])
        )
    value = dot(tokens[...], qkv_w[:, :D], 1, 0) + span(BIAS_QUERY)
    query[...] = value.astype(bf16)
    query_turned[...] = transposed(query[...])
    allowed = allowed_mask(row_class, lengths, 2 * y + core, tok)
    masks, first = half_masks()
    tokens_came = share_half(tokens, narrow_tokens)
    for copy in kv_came:
        copy.wait_recv()

    scale = HEAD_DIM ** (-0.5)

    def lanes_at(start):
        return pl.ds(pl.multiple_of(start, LANES), LANES)

    def attend_pair(pair, carry):
        cols = lanes_at(pair * LANES)
        keys = keys_values[:, cols]
        values = keys_values[:, lanes_at(D + pair * LANES)]
        outs = []
        for side, mask in enumerate(masks):
            score = dot(query[:, cols] * (mask * scale), keys, 1, 1)
            score = jnp.where(allowed, score, masked_score)
            exponent = jnp.exp(score - jnp.max(score, axis=-1, keepdims=True))
            chance = exponent * (1.0 / jnp.sum(exponent, axis=-1, keepdims=True))
            chance = chance.astype(bf16)
            prob[2 * pair + side] = chance
            outs.append(dot(chance, values, 1, 0))
        attended[:, cols] = jnp.where(first, outs[0], outs[1]).astype(bf16)
        return carry

    lax.fori_loop(0, HEADS // 2, attend_pair, 0)
    attended_came = share_half(attended, narrow_attended)

    loads["out"].wait()
    work[...] = dot(attended[...], out_w[...], 1, 0)

    def norm_one(rows, carry):
        value = tokens[rows, :].astype(f32) + (work[rows, :] + span(BIAS_OUT))
        centre = value - row_mean(value)
        rstd = lax.rsqrt(row_mean(centre * centre) + norm_eps)
        zhat = centre * rstd
        normed = zhat * span(GAIN_ONE) + span(SHIFT_ONE)
        zhat_one[rows, :] = zhat
        rstd_one[rows, :] = jnp.broadcast_to(rstd, (ROWS, LANES))
        normed_one[rows, :] = normed
        normed_low[rows, :] = normed.astype(bf16)
        return carry

    by_rows(tok, norm_one)
    normed_came = share_half(normed_low, narrow_normed)

    loads["up"].wait()
    for tile in range(FF // D):
        cols = slice(tile * D, (tile + 1) * D)
        work[...] = dot(normed_low[...], up_w[:, cols], 1, 0)

        def gelu(rows, carry):
            value = work[rows, :] + span(BIAS_UP + cols.start)
            chance, density = normal_parts(value)
            active[rows, cols] = (value * chance).astype(bf16)
            slope[rows, cols] = chance + value * density
            return carry

        by_rows(tok, gelu)
    active_came = to_partner(active.at[own_rows], active.at[far_rows])
    loads["down"].wait()
    work[...] = dot(active[own_rows, :], down_w[...], 1, 0)

    def norm_two(rows, carry):
        value = normed_one[rows, :] + (work[rows, :] + span(BIAS_DOWN))
        centre = value - row_mean(value)
        rstd = lax.rsqrt(row_mean(centre * centre) + norm_eps)
        zhat = centre * rstd
        mixed[rows, :] = zhat * span(GAIN_TWO) + span(SHIFT_TWO)
        grad = cotangent[rows, :].astype(f32)
        inner = grad * span(GAIN_TWO)
        grad_in = (inner - row_mean(inner) - zhat * row_mean(inner * zhat)) * rstd
        grad_two[rows, :] = grad_in
        low = grad_in.astype(bf16)
        grad_down[rows, :] = low
        gain, shift, bias = carry
        return gain + fold(grad * zhat), shift + fold(grad), bias + fold(low.astype(f32))

    zero = jnp.zeros((8, D), f32)
    gain, shift, bias = by_rows(tok, norm_two, (zero, zero, zero))
    put_vec(GAIN_TWO, column_sum(gain))
    put_vec(SHIFT_TWO, column_sum(shift))
    put_vec(BIAS_DOWN, column_sum(bias))
    grad_down_came = share_half(grad_down, narrow_grad)
    keys_turned[...] = transposed(keys_values[:, :D])

    here = {"f": z // 2, "n": z % 2, "x": x, "y": y}
    across = {"f": along[1], "n": along[0], "x": beside, "y": beyond}

    class Chain:
        def __init__(self, index):
            matrix, start, rows, order = CHUNKS[index]
            self.index, self.order, self.stage = index, order, 0
            self.rows = pl.ds(start, rows)
            self.own = part.at[matrix]
            self.came = [ref.at[matrix] for ref in (came_one, came_two, came_three, came_four)]
            self.final = sums.at[matrix]

        def cells(self, free, flipped=None):
            return tuple(
                slice(None) if name in free else 1 - here[name] if name == flipped else here[name]
                for name in "fnxy"
            ) + (self.rows,)

        def send(self, source, target, other):
            sems = (send_sem.at[self.index, self.stage], recv_sem.at[self.index, self.stage])
            self.copy = remote(source, target, *sems, other)

        def advance(self):
            stage, order = self.stage, self.order
            if stage:
                self.copy.wait_recv()
            if 1 <= stage <= 4:
                free = order[stage:]
                for choice in itertools.product((0, 1), repeat=len(free)):
                    taken = dict(zip(sorted(free, key="fnxy".index), choice))
                    at = tuple(taken.get(name, here[name]) for name in "fnxy") + (self.rows,)
                    value = self.own[at] + self.came[stage - 1][choice + (self.rows,)]
                    if stage == 4:
                        self.final[core, y, self.rows] = value
                    else:
                        self.own[at] = value
            if stage < 4:
                name = order[stage]
                source = self.own.at[self.cells(order[stage + 1 :], name)]
                target = self.came[stage].at[(slice(None),) * (3 - stage) + (self.rows,)]
                self.send(source, target, across[name])
            elif stage == 4:
                block = self.final.at[core, y, self.rows]
                self.send(block, block, beyond)
            elif stage == 5:
                block = self.final.at[core, :, self.rows]
                self.send(block, block, partner)
            self.stage += 1

    chains = [Chain(index) for index in range(len(CHUNKS))]
    plan = iter(CHUNK_PLAN)

    def pump():
        for index in next(plan):
            chains[index].advance()

    def feed_forward(matrix, narrow, wide):
        left = transposed(narrow[...])

        def block(index, carry):
            cols = pl.ds(pl.multiple_of(index * UNIT, UNIT), UNIT)
            value = dot(left, wide[:, cols], 1, 0).astype(bf16)
            for side in range(2):
                part[matrix, index // 4, index // 2 % 2, index % 2, side] = value[
                    side * SIDE : (side + 1) * SIDE
                ]
            return carry

        lax.fori_loop(0, 8, block, 0)

    def projections(matrix, turned, narrow, width, offset, between=None):
        for tile in range(turned.shape[0] // UNIT):
            if between and tile % 2 == 0:
                between()
            value = dot(turned[tile * UNIT : (tile + 1) * UNIT, :], narrow[...], 1, 0).astype(bf16)
            for start in range(0, UNIT, PIECE):
                block, row = divmod(tile * UNIT + start, width)
                side, row = divmod(offset + row, SIDE)
                cell = (matrix, block // 4, block // 2 % 2, block % 2, side)
                part[cell + (pl.ds(row, PIECE),)] = value[start : start + PIECE]

    grad_down_came.wait_recv()
    active_came.wait_recv()
    feed_forward(0, narrow_grad, active)

    for tile in range(FF // D):
        pump()
        cols = slice(tile * D, (tile + 1) * D)
        work[...] = dot(grad_down[...], down_w[cols, :], 1, 1)

        def gelu_back(rows, carry):
            low = (work[rows, :] * slope[rows, cols]).astype(bf16)
            grad_up[rows, cols] = low
            return carry + fold(low.astype(f32))

        put_vec(BIAS_UP + cols.start, column_sum(by_rows(tok, gelu_back, zero)))
    grad_up_came = to_partner(grad_up.at[own_rows], grad_up.at[far_rows])
    pump()
    normed_came.wait_recv()
    grad_up_came.wait_recv()
    feed_forward(1, narrow_normed, grad_up)
    pump()

    work[...] = dot(grad_up[own_rows, :], up_w[...], 1, 1)

    def norm_one_back(rows, carry):
        grad = grad_two[rows, :] + work[rows, :]
        zhat = zhat_one[rows, :]
        inner = grad * span(GAIN_ONE)
        grad_in = inner - row_mean(inner) - zhat * row_mean(inner * zhat)
        grad_in = grad_in * rstd_one[rows, 0:1]
        grad_one[rows, :] = grad_in
        low = grad_in.astype(bf16)
        grad_attn[rows, :] = low
        gain, shift, bias = carry
        return gain + fold(grad * zhat), shift + fold(grad), bias + fold(low.astype(f32))

    gain, shift, bias = by_rows(tok, norm_one_back, (zero, zero, zero))
    put_vec(GAIN_ONE, column_sum(gain))
    put_vec(SHIFT_ONE, column_sum(shift))
    put_vec(BIAS_OUT, column_sum(bias))
    grad_heads[...] = dot(grad_attn[...], out_w[...], 1, 1).astype(bf16)
    heads_turned[...] = dot(out_w[...], grad_attn[...], 1, 1).astype(bf16)

    half_lanes = LANES // 2

    def attend_pair_back(pair, carry):
        cols = lanes_at(pair * LANES)
        values = keys_values[:, lanes_at(D + pair * LANES)]
        for side, mask in enumerate(masks):
            start = pl.multiple_of(pair * LANES + side * half_lanes, half_lanes)
            rows = pl.ds(start, half_lanes)
            low_chance = prob[2 * pair + side]
            chance = low_chance.astype(f32)
            grad_chance = dot(grad_heads[:, cols] * mask, values, 1, 1)
            mean = jnp.sum(chance * grad_chance, axis=-1, keepdims=True)
            grad_score = (chance * (grad_chance - mean)).astype(bf16)
            values_grad = dot(heads_turned[rows, :], low_chance, 1, 0).astype(bf16)
            keys_grad = (dot(query_turned[rows, :], grad_score, 1, 0) * scale).astype(bf16)
            query_grad = (dot(keys_turned[rows, :], grad_score, 1, 1) * scale).astype(bf16)
            blocks = (
                query_grad,
                keys_grad[:, :tok],
                values_grad[:, :tok],
                keys_grad[:, tok:],
                values_grad[:, tok:],
            )
            for index, value in enumerate(blocks):
                start = index * LANES + side * half_lanes
                exchanged[0, pair, start : start + half_lanes, :] = value
        return carry

    half_came = []
    for half in range(2):
        pump()
        pairs = pl.ds(half * HEADS // 4, HEADS // 4)
        lax.fori_loop(half * HEADS // 4, (half + 1) * HEADS // 4, attend_pair_back, 0)
        half_came.append(to_partner(exchanged.at[0, pairs], exchanged.at[1, pairs]))
    pump()
    attn_turned[:, own_lanes] = transposed(grad_attn[...])
    grad_attn_came = to_partner(attn_turned.at[:, own_lanes], attn_turned.at[:, far_lanes])

    for pair in range(HEADS // 2):
        if pair % (HEADS // 4) == 0:
            half_came[pair // (HEADS // 4)].wait_recv()
        for who, lanes in enumerate((own_lanes, far_lanes)):
            start = pair * LANES
            mine, theirs = exchanged.at[who, pair], exchanged.at[1 - who, pair]
            qkv_turned[start : start + LANES, lanes] = mine[:LANES]
            for index in (1, 2):
                rows = slice(index * LANES, (index + 1) * LANES)
                sent = slice((index + 2) * LANES, (index + 3) * LANES)
                value = mine[rows].astype(f32) + theirs[sent].astype(f32)
                start = index * D + pair * LANES
                qkv_turned[start : start + LANES, lanes] = value.astype(bf16)
    pump()
    tokens_came.wait_recv()
    projections(2, qkv_turned, narrow_tokens, 3 * D // 8, 0, pump)
    attended_came.wait_recv()
    grad_attn_came.wait_recv()
    projections(2, attn_turned, narrow_attended, D // 8, 3 * D // 8)
    pump()

    ones = jnp.ones((8, tok), bf16)
    for start, rows in ((BIAS_QUERY, slice(0, D)), (BIAS_VALUE, slice(2 * D, 3 * D))):
        put_vec(start, dot(ones, qkv_turned[rows, own_lanes], 1, 1)[0:1])
    vec_came = to_partner(vec, vec_core)
    value = dot(qkv_w[...], qkv_turned[:, own_lanes], 1, 0)
    input_grad[...] = grad_one[...] + value.T

    vec_slots = [(send_sem.at[len(CHUNKS), i], recv_sem.at[len(CHUNKS), i]) for i in range(5)]

    def vec_steps():
        vec_came.wait_recv()
        vec_core[...] = vec[...] + vec_core[...]
        copy = remote(vec_core, vec_y, *vec_slots[0], beyond)
        yield
        copy.wait_recv()
        for i in range(4):
            vec_x[0, i] = vec_core[2 * i + x] + vec_y[2 * i + x]
            vec_x[1, i] = vec_core[2 * i + 1 - x] + vec_y[2 * i + 1 - x]
        copy = remote(vec_x.at[1], vec_x.at[2], *vec_slots[1], beside)
        yield
        copy.wait_recv()
        vec_x[0] = vec_x[0] + vec_x[2]
        copies = [
            remote(
                vec_x.at[0, flip_z(z, step)],
                vec_z.at[step - 1],
                *vec_slots[1 + step],
                along[step - 1],
            )
            for step in (1, 2, 3)
        ]
        yield
        total = vec_x[0, z]
        for step, copy in enumerate(copies):
            copy.wait_recv()
            total = total + vec_z[step]
        vec_sum[...] = total
        yield

    steps = vec_steps()
    for turn, index in enumerate(next(plan)):
        chains[index].advance()
        if turn % 10 == 9 and turn < 40:
            next(steps)
    for copy in started:
        copy.wait_send()


def layer(row_class, lengths, tokens, cotangent, vectors, qkv_w, out_w, up_w, down_w):
    tok = tokens.shape[0]
    side = (SIDE, UNIT)

    def low(*dims):
        return pltpu.VMEM(dims, bf16)

    def wide(*dims):
        return pltpu.VMEM(dims, f32)

    return pl.pallas_call(
        layer_kernel,
        out_shape=(
            jax.ShapeDtypeStruct((tok, D), f32),
            jax.ShapeDtypeStruct((tok, D), f32),
            jax.ShapeDtypeStruct((3, 2, 2) + side, bf16),
            jax.ShapeDtypeStruct((16, LANES), f32),
        ),
        in_specs=[SMEM, SMEM, VMEM, VMEM, VMEM] + [ANY] * 4,
        out_specs=(VMEM,) * 4,
        scratch_shapes=[
            low(D, 3 * D),
            low(D, D),
            low(D, FF),
            low(FF, D),
            low(tok, D),
            low(D, tok),
            low(2 * tok, 2 * D),
            low(D, 2 * tok),
            low(HEADS, tok, 2 * tok),
            low(tok, D),
            low(tok, D),
            low(tok, D),
            low(tok, D),
            low(2 * tok, HALF),
            low(2 * tok, HALF),
            low(2 * tok, HALF),
            low(2 * tok, HALF),
            low(2 * tok, FF),
            low(2 * tok, FF),
            low(D, 2 * tok),
            low(3 * D, 2 * tok),
            low(2, HEADS // 2, 5 * LANES, tok),
            low(tok, D),
            low(D, tok),
            wide(tok, FF),
            wide(tok, D),
            wide(tok, D),
            wide(tok, LANES),
            wide(tok, D),
            wide(tok, D),
            wide(8, 16, LANES),
            wide(8, 16, LANES),
            wide(8, 16, LANES),
            wide(3, 4, 16, LANES),
            wide(3, 16, LANES),
            low(3, 2, 2, 2, 2, *side),
            low(3, 2, 2, 2, *side),
            low(3, 2, 2, *side),
            low(3, 2, *side),
            low(3, *side),
            pltpu.SemaphoreType.DMA((4,)),
            pltpu.SemaphoreType.DMA((12,)),
            pltpu.SemaphoreType.DMA((12,)),
            pltpu.SemaphoreType.DMA((len(CHUNKS) + 1, 6)),
            pltpu.SemaphoreType.DMA((len(CHUNKS) + 1, 6)),
        ],
        compiler_params=pltpu.CompilerParams(
            vmem_limit_bytes=63 * MIB, collective_id=0, has_side_effects=True
        ),
        name="layer",
    )(row_class, lengths, tokens, cotangent, vectors[None, :], qkv_w, out_w, up_w, down_w)


GRAM_AXES = ("far", "near", "x")
GRAM_GROUPS = (
    (1, "xnf"),
    (2, "xnf"),
    (2, "xnf"),
    (3, "xnf"),
    (3, "nxf"),
    (3, "fxn"),
    (3, "nxf"),
    (2, "xnf"),
    (1, "xnf"),
    (1, "xnf"),
)
GRAM_PLAN = (
    6, 0, 9, 2, 5, 4, 7, 3, 0, 9, 6, 8, 2, 0, 9, 1, 0, 7, 9, 8, 2, 6,
    0, 5, 4, 3, 1, 8, 2, 7, 0, 6, 9, 5, 4, 8, 0, 2, 7, 1, 8, 9, 6, 3,
    5, 4, 7, 1, 8, 6, 2, 9, 3, 5, 8, 1, 4, 7, 2, 3, 5, 1, 4, 6, 7, 3,
    1, 5, 3, 4,
)


def muon_kernel(
    sums,
    qkv_hbm,
    out_hbm,
    up_hbm,
    down_hbm,
    factors,
    own_sum,
    qkv_old,
    out_old,
    old,
    moment,
    out,
    part,
    came_one,
    came_two,
    came_three,
    high,
    low,
    load_sem,
    send_sem,
    recv_sem,
    share_send,
    share_recv,
    *ortho,
):
    z, x, y, core = position()
    here = {"far": z // 2, "near": z % 2, "x": x}
    others = {
        "far": device(flip_z(z, 2), x, y, core),
        "near": device(flip_z(z, 1), x, y, core),
        "x": device(z, 1 - x, y, core),
    }
    beyond = device(z, x, 1 - y, core)
    partner = device(z, x, y, 1 - core)
    own = 2 * y + core
    all_here = greet(list(others.values()) + [beyond, partner])

    def load_two(source, target, matrix):
        loads = [
            pltpu.make_async_copy(source, target, load_sem.at[0]),
            pltpu.make_async_copy(sums.at[matrix], own_sum, load_sem.at[1]),
        ]
        for load in loads:
            load.start()
        for load in loads:
            load.wait()

    def from_turned(source, target, skip):
        load_two(source, target, 2)
        rows = target.shape[0]
        moment[...] = jnp.zeros_like(moment)
        for half in range(2):
            cols = slice(half * HALF, (half + 1) * HALF)
            start = half * UNIT + skip
            value = own_sum[start : start + rows, :].astype(f32)
            moment[cols, skip : skip + rows] = (muon_keep * target[:, cols] + value).T

    @pl.when(own == 0)
    def _():
        from_turned(qkv_hbm, qkv_old, 0)

    @pl.when(own == 1)
    def _():
        from_turned(out_hbm, out_old, qkv_old.shape[0])

    @pl.when(own == 2)
    def _():
        load_two(up_hbm, old, 1)
        moment[...] = muon_keep * old[...] + own_sum[...].astype(f32)

    @pl.when(own == 3)
    def _():
        load_two(down_hbm, old, 0)
        moment[...] = muon_keep * old[...] + own_sum[...].astype(f32)

    all_here()
    blocks = sub_blocks(moment.shape[0])
    starts = [sum(count for count, _ in GRAM_GROUPS[:group]) for group in range(len(GRAM_GROUPS))]
    high[...] = moment[...].astype(bf16)
    low[...] = (moment[...] - high[...].astype(f32)).astype(bf16)
    started = []

    def product(index):
        i, j = blocks[index]
        left, right = pl.ds(i * SUB, SUB), pl.ds(j * SUB, SUB)
        total = dot(high[left, :], high[right, :], 1, 1)
        total = total + dot(high[left, :], low[right, :], 1, 1)
        total = total + dot(low[left, :], high[right, :], 1, 1)
        rows = SUB // 8
        for owner in range(8):
            cell = (owner // 4, owner // 2 % 2, owner % 2)
            part[cell + (index,)] = total[
                owner * rows : (owner + 1) * rows
            ]

    def send(source, target, group, slot, axis):
        copy = pltpu.make_async_remote_copy(
            src_ref=source,
            dst_ref=target,
            send_sem=send_sem.at[group, slot],
            recv_sem=recv_sem.at[group, slot],
            device_id=others[axis],
            device_id_type=MESH,
        )
        copy.start()
        started.append(copy)
        return copy

    def cells(fixed, flipped=None):
        return tuple(
            1 - here[name] if name == flipped else here[name] if name in fixed else slice(None)
            for name in GRAM_AXES
        )

    class Walk:
        def __init__(self, group):
            count, order = GRAM_GROUPS[group]
            self.group, self.stage = group, 0
            self.order = [GRAM_AXES["fnx".index(letter)] for letter in order]
            self.mine = (pl.ds(starts[group], count),)
            self.came = [
                ref.at[(slice(None),) * (2 - stage) + self.mine]
                for stage, ref in enumerate((came_one, came_two, came_three))
            ]

        def advance(self):
            stage, order = self.stage, self.order
            mine = self.mine
            if stage:
                self.copy.wait_recv()
            if 1 <= stage <= 3:
                kept = cells(order[:stage]) + mine
                total = part[kept] + self.came[stage - 1][...]
                if stage == 3:
                    out[kept] = total
                else:
                    part[kept] = total
            if stage < 3:
                source = part.at[cells(order[:stage], order[stage]) + mine]
                self.copy = send(source, self.came[stage], self.group, stage, order[stage])
            elif stage < 6:
                block = out.at[cells(order[: 6 - stage]) + mine]
                self.copy = send(block, block, self.group, stage, order[5 - stage])
            self.stage += 1

    walks = [Walk(group) for group in range(len(GRAM_GROUPS))]
    for group in GRAM_PLAN:
        if walks[group].stage == 0:
            for index in range(starts[group], starts[group] + GRAM_GROUPS[group][0]):
                product(index)
        walks[group].advance()

    e = ortho[0]
    for index, (i, j) in enumerate(blocks):
        value = out[:, :, :, index].reshape(SUB, SUB)
        e[i * SUB : (i + 1) * SUB, j * SUB : (j + 1) * SUB] = value
        if i != j:
            e[j * SUB : (j + 1) * SUB, i * SUB : (i + 1) * SUB] = value.T

    across, beside = [], []

    def share(slot, rows, kind, other):
        block = factors.at[slot, rows]
        index = rows.start // TILE
        copy = pltpu.make_async_remote_copy(
            src_ref=block,
            dst_ref=block,
            send_sem=share_send.at[index, kind],
            recv_sem=share_recv.at[index, kind],
            device_id=other,
            device_id_type=MESH,
        )
        copy.start()
        started.append(copy)
        return copy

    def emit(rows, value):
        factors[own, rows, :] = value
        across.append((rows, share(own, rows, 0, beyond)))
        beside.append(share(own, rows, 1, partner))

    newton_schulz(e, moment, *ortho, emit)
    for rows, copy in across:
        copy.wait_recv()
        beside.append(share(2 * (1 - y) + core, rows, 2, partner))
    for copy in beside:
        copy.wait_recv()
    for copy in started:
        copy.wait_send()


def muon_factors(sums, *olds):
    size, cols = olds[2].shape
    count = len(sub_blocks(size))
    groups = len(GRAM_GROUPS)
    rows = (SUB // 8, SUB)

    def wide(*dims):
        return pltpu.VMEM(dims, f32)

    return pl.pallas_call(
        muon_kernel,
        out_shape=jax.ShapeDtypeStruct((4, size, cols), bf16),
        in_specs=[ANY] * 5,
        out_specs=VMEM,
        scratch_shapes=[
            pltpu.VMEM((size, cols), bf16),
            wide(*olds[0].shape),
            wide(*olds[1].shape),
            wide(size, cols),
            wide(size, cols),
            wide(2, 2, 2, count, *rows),
            wide(2, 2, 2, count, *rows),
            wide(2, 2, count, *rows),
            wide(2, count, *rows),
            wide(count, *rows),
            pltpu.VMEM((size, cols), bf16),
            pltpu.VMEM((size, cols), bf16),
            pltpu.SemaphoreType.DMA((2,)),
            pltpu.SemaphoreType.DMA((groups, 6)),
            pltpu.SemaphoreType.DMA((groups, 6)),
            pltpu.SemaphoreType.DMA((size // TILE, 3)),
            pltpu.SemaphoreType.DMA((size // TILE, 3)),
        ]
        + ortho_scratch(size, cols),
        compiler_params=pltpu.CompilerParams(
            vmem_limit_bytes=58 * MIB, collective_id=1, has_side_effects=True
        ),
        name="muon_factors",
    )(sums, *olds)


def window(start, width, total):
    size = -(-(width + 96) // LANES) * LANES
    first = jnp.minimum(start // LANES * LANES, total - size)
    return pl.ds(pl.multiple_of(first, LANES), size), start - first


def finish_kernel(
    factors_hbm,
    sums_hbm,
    qkv_hbm,
    out_hbm,
    up_hbm,
    down_hbm,
    qkv_old_hbm,
    out_old_hbm,
    up_old_hbm,
    down_old_hbm,
    mixed_hbm,
    grad_hbm,
    mixed_out,
    grad_out,
    qkv_moment_out,
    out_moment_out,
    up_moment_out,
    down_moment_out,
    qkv_out,
    out_out,
    up_out,
    down_out,
    factors,
    sums,
    qkv_w,
    out_w,
    up_w,
    down_w,
    qkv_moment,
    out_moment,
    up_moment,
    down_moment,
    qkv_new,
    out_new,
    up_new,
    down_new,
    turned,
    load_sem,
    store_sem,
):
    shrink = 1.0 - muon_rate * muon_decay
    dp_id = lax.axis_index("dp")
    qkv_cols, out_cols = qkv_new.shape[0], out_new.shape[0]
    qkv_lanes, qkv_skip = window(dp_id * qkv_cols, qkv_cols, 3 * D)
    out_lanes, out_skip = window(dp_id * out_cols, out_cols, D)
    block = pl.ds(pl.multiple_of(dp_id * UNIT, UNIT), UNIT)
    pairs = {
        "sums": (sums_hbm, sums),
        "up_moment": (up_old_hbm, up_moment),
        "down_moment": (down_old_hbm, down_moment),
        "factors": (factors_hbm, factors),
        "up": (up_hbm.at[:, block], up_w),
        "down": (down_hbm.at[block], down_w),
        "qkv_moment": (qkv_old_hbm, qkv_moment),
        "out_moment": (out_old_hbm, out_moment),
        "qkv": (qkv_hbm.at[:, qkv_lanes], qkv_w),
        "out": (out_hbm.at[:, out_lanes], out_w),
    }
    loads = {
        name: pltpu.make_async_copy(source, target, load_sem.at[index])
        for index, (name, (source, target)) in enumerate(pairs.items())
    }
    for load in loads.values():
        load.start()
    stores = []

    def store(source, target):
        stores.append(pltpu.make_async_copy(source, target, store_sem.at[len(stores)]))
        stores[-1].start()

    store(mixed_hbm, mixed_out)
    store(grad_hbm, grad_out)

    def step(index, rate):
        return muon_rate * rate * factors[index].astype(f32)

    loads["sums"].wait()
    for index, name, target, out in (
        (1, "up_moment", up_moment, up_moment_out),
        (0, "down_moment", down_moment, down_moment_out),
    ):
        loads[name].wait()
        target[...] = muon_keep * target[...] + sums[index].astype(f32)
        store(target, out)
    loads["qkv_moment"].wait()
    loads["out_moment"].wait()
    for half in range(2):
        cols = slice(half * HALF, (half + 1) * HALF)
        value = sums[2, cols].astype(f32)
        qkv_moment[:, cols] = muon_keep * qkv_moment[:, cols] + value[:qkv_cols]
        out_moment[:, cols] = muon_keep * out_moment[:, cols] + value[qkv_cols:]
    store(qkv_moment, qkv_moment_out)
    store(out_moment, out_moment_out)
    loads["factors"].wait()
    loads["up"].wait()
    up_new[...] = up_w[...].astype(f32) * shrink - step(2, math.sqrt(max(1.0, FF / D)))
    store(up_new, up_out)
    loads["down"].wait()
    down_new[...] = down_w[...].astype(f32) * shrink - step(3, 1.0).T
    store(down_new, down_out)
    loads["qkv"].wait()
    turned[...] = qkv_w[...].astype(f32).T
    rows = pl.ds(pl.multiple_of(qkv_skip, 32), qkv_cols)
    qkv_new[...] = turned[rows, :] * shrink - step(0, math.sqrt(3.0)).T[:qkv_cols]
    store(qkv_new, qkv_out)
    loads["out"].wait()
    turned[: out_w.shape[1], :] = out_w[...].astype(f32).T
    rows = pl.ds(pl.multiple_of(out_skip, 32), out_cols)
    out_new[...] = turned[rows, :] * shrink - step(1, 1.0).T[qkv_cols:]
    store(out_new, out_out)
    for copy in stores:
        copy.wait()


def finish(factors, sums, weights, olds, mixed, input_grad):
    shapes = [old.shape for old in olds]
    news = shapes[:3] + [shapes[3][::-1]]

    def wide(shape):
        return pltpu.VMEM(shape, f32)

    return pl.pallas_call(
        finish_kernel,
        out_shape=tuple(
            jax.ShapeDtypeStruct(shape, f32)
            for shape in [mixed.shape, input_grad.shape] + shapes + news
        ),
        in_specs=[ANY] * 12,
        out_specs=(ANY,) * 10,
        scratch_shapes=[
            pltpu.VMEM(factors.shape, bf16),
            pltpu.VMEM(sums.shape, bf16),
            pltpu.VMEM((D, 384), bf16),
            pltpu.VMEM((D, 256), bf16),
            pltpu.VMEM((D, UNIT), bf16),
            pltpu.VMEM((UNIT, D), bf16),
        ]
        + [wide(shape) for shape in shapes + news]
        + [
            wide((384, D)),
            pltpu.SemaphoreType.DMA((10,)),
            pltpu.SemaphoreType.DMA((10,)),
        ],
        compiler_params=pltpu.CompilerParams(vmem_limit_bytes=48 * MIB),
        name="finish",
    )(factors, sums, *weights, *olds, mixed, input_grad)


def swap(value, axis, bit):
    size = lax.axis_size(axis)
    return lax.ppermute(value, axis, [(i, i ^ bit) for i in range(size)])


def scatter_head(value, bit, position):
    half = value.shape[1] // 2
    mine = lax.dynamic_slice_in_dim(value, position * half, half, 1)
    other = lax.dynamic_slice_in_dim(value, (1 - position) * half, half, 1)
    return (mine.astype(f32) + swap(other, "head", bit).astype(f32)).astype(bf16)


def scatter_dp_pair(value, position):
    paired = value.reshape((value.shape[0] // 2, 2) + value.shape[1:])
    mine = lax.dynamic_index_in_dim(paired, position, 1, False)
    other = lax.dynamic_index_in_dim(paired, 1 - position, 1, False)
    return (mine.astype(f32) + swap(other, "dp", 1).astype(f32)).astype(bf16)


def scatter_dp_rest(value, place):
    ranks = value.shape[0]
    total = lax.dynamic_index_in_dim(value, place, 0, False).astype(f32)
    for step in range(1, ranks):
        sent = lax.dynamic_index_in_dim(value, place ^ step, 0, False)
        total = total + swap(sent, "dp", 2 * step).astype(f32)
    return total


def local(
    tokens,
    cotangent,
    qkv_weight,
    out_weight,
    up_weight,
    down_weight,
    vectors,
    qkv_moment,
    out_moment,
    up_moment,
    down_moment,
    adam_first,
    adam_second,
    bucket_class,
    row_lengths,
):
    n_dp = lax.axis_size("dp")
    n_head = lax.axis_size("head")
    dp_id = lax.axis_index("dp")
    head_id = lax.axis_index("head")
    core, side = head_id % 2, head_id // 2
    tok, width = tokens.shape
    hidden = up_weight.shape[1]
    half = width // 2
    qkv_cols, out_cols = qkv_moment.shape[1], out_moment.shape[1]
    shrink = 1.0 - muon_rate * muon_decay

    def weight_block(weight, cols, dim):
        return lax.dynamic_slice_in_dim(weight, dp_id * cols, cols, dim)

    block = head_id.astype(jnp.int32)[None]
    vec_len = vectors.shape[0] // n_dp
    if (n_dp, n_head, tok) == (8, 4, 256):
        mixed, input_grad, sums, vec = layer(
            bucket_class,
            row_lengths,
            tokens,
            cotangent,
            vectors,
            qkv_weight,
            out_weight,
            up_weight,
            down_weight,
        )
        grad_vec = vec[:VEC_BLOCK].reshape(vec_len)
        sums = sums.reshape(3, width, -1)
        olds = [qkv_moment.T, out_moment.T, up_moment, down_moment]
        mixed, input_grad, *results = finish(
            muon_factors(sums, *olds),
            sums,
            [qkv_weight, out_weight, up_weight, down_weight],
            olds,
            mixed,
            input_grad,
        )
        moments, new_weights = results[:4], results[4:]
        moments = [moments[0].T, moments[1].T, *moments[2:]]
        new_weights = [new_weights[0].T, new_weights[1].T, *new_weights[2:]]
    else:
        pieces = split_vectors(vectors, width, hidden)
        bias_query, bias_value, bias_out, gain_one, shift_one = pieces[:5]
        bias_up, bias_down, gain_two, shift_two = pieces[5:]
        bias_qkv = jnp.concatenate([bias_query, jnp.zeros_like(bias_query), bias_value])

        def column_half(value, which):
            return lax.dynamic_slice_in_dim(value, which * half, half, 1)

        qkv = (dot(tokens, qkv_weight, 1, 0) + bias_qkv).astype(bf16)
        other = swap(qkv[:, width:], "head", 1)
        attended = attend(block, bucket_class, row_lengths, qkv, other)
        attn_val = dot(attended, out_weight, 1, 0) + bias_out
        resid_one = tokens.astype(f32) + attn_val
        centre = resid_one - jnp.mean(resid_one, axis=-1, keepdims=True)
        rstd_one = lax.rsqrt(jnp.mean(centre * centre, axis=-1, keepdims=True) + norm_eps)
        zhat_one = centre * rstd_one
        normed_one = zhat_one * gain_one + shift_one
        normed_low = normed_one.astype(bf16)
        up_val = dot(normed_low, up_weight, 1, 0) + bias_up
        phi_cum = 0.5 * (1.0 + lax.erf(up_val * (0.5**0.5)))
        active_low = (up_val * phi_cum).astype(bf16)
        slope = phi_cum + up_val * jnp.exp(-0.5 * up_val * up_val) * (1.0 / math.sqrt(2.0 * math.pi))
        down_val = dot(active_low, down_weight, 1, 0) + bias_down
        resid_two = normed_one + down_val
        centre = resid_two - jnp.mean(resid_two, axis=-1, keepdims=True)
        rstd_two = lax.rsqrt(jnp.mean(centre * centre, axis=-1, keepdims=True) + norm_eps)
        zhat_two = centre * rstd_two
        mixed = zhat_two * gain_two + shift_two

        def norm_back(grad, gain, zhat, rstd):
            inner = grad * gain
            mean = jnp.mean(inner, axis=-1, keepdims=True)
            slant = jnp.mean(inner * zhat, axis=-1, keepdims=True)
            return (inner - mean - zhat * slant) * rstd, jnp.sum(grad * zhat, axis=0), jnp.sum(grad, axis=0)

        grad_two, grad_gain_two, grad_shift_two = norm_back(
            cotangent.astype(f32), gain_two, zhat_two, rstd_two
        )
        grad_down_low = grad_two.astype(bf16)
        grad_bias_down = jnp.sum(grad_down_low, axis=0, dtype=f32)

        x_id, z_id = dp_id % 2, dp_id // 2

        grad_up_low = (dot(grad_down_low, down_weight, 1, 1) * slope).astype(bf16)
        grad_bias_up = jnp.sum(grad_up_low, axis=0, dtype=f32)
        grad_normed = grad_two + dot(grad_up_low, up_weight, 1, 1)
        grad_one, grad_gain_one, grad_shift_one = norm_back(grad_normed, gain_one, zhat_one, rstd_one)
        grad_attn_low = grad_one.astype(bf16)
        grad_bias_out = jnp.sum(grad_attn_low, axis=0, dtype=f32)
        grad_heads = dot(grad_attn_low, out_weight, 1, 1).astype(bf16)
        grad_query, own, sent = attend_back(block, bucket_class, row_lengths, qkv, other, grad_heads)
        grad_kv = (own + swap(sent, "head", 1).astype(f32)).astype(bf16)
        grad_qkv = jnp.concatenate([grad_query, grad_kv], axis=1)
        grad_bias_qkv = jnp.sum(grad_qkv, axis=0, dtype=f32)
        input_grad = grad_one + dot(grad_qkv, qkv_weight, 1, 1)
        grad_vector = jnp.concatenate(
            [
                grad_bias_qkv[:width],
                grad_bias_qkv[2 * width :],
                grad_bias_out,
                grad_gain_one,
                grad_shift_one,
                grad_bias_up,
                grad_bias_down,
                grad_gain_two,
                grad_shift_two,
            ]
        )
        grad_vector = grad_vector + swap(grad_vector, "head", 1)
        wides = [active_low, grad_up_low, grad_attn_low, grad_qkv]
        narrows = [grad_down_low, normed_low, attended, tokens]

        def both_halves(value):
            return jnp.concatenate(
                [column_half(value, core), swap(column_half(value, 1 - core), "head", 1)], axis=0
            )

        def weight_grad(wide, narrow):
            wide = jnp.concatenate([wide, swap(wide, "head", 1)], axis=0)
            value = dot(wide, both_halves(narrow), 0, 0).astype(bf16)
            return value.reshape(n_dp, value.shape[0] // n_dp, half)

        def reduce_y_first(value):
            return scatter_dp_rest(scatter_dp_pair(scatter_head(value, 2, side), x_id), z_id)

        def reduce_x_first(value):
            return scatter_dp_rest(scatter_head(scatter_dp_pair(value, x_id), 2, side), z_id)

        def spread(value):
            value = value.astype(bf16)
            came = swap(value, "head", 2)
            value = jnp.concatenate(
                [jnp.where(side == 0, value, came), jnp.where(side == 0, came, value)], axis=0
            )
            came = swap(value, "head", 1)
            return jnp.concatenate(
                [jnp.where(core == 0, value, came), jnp.where(core == 0, came, value)], axis=1
            ).astype(f32)

        down_part, up_part, out_part, qkv_part = [
            weight_grad(wide, narrow) for wide, narrow in zip(wides, narrows)
        ]
        vec_rows = 16
        vec_part = grad_vector.reshape(n_dp, vec_len)
        vec_part = jnp.pad(vec_part, ((0, 0), (0, vec_rows * width - vec_len)))
        vec_part = vec_part.reshape(n_dp, vec_rows, width)
        vec_part = lax.dynamic_slice_in_dim(vec_part, core * half, half, 2).astype(bf16)
        down_new = spread(reduce_x_first(down_part))
        up_new = spread(reduce_y_first(up_part))
        tail_new = spread(
            reduce_y_first(jnp.concatenate([qkv_part, out_part, vec_part], axis=1))
        )
        grads = [
            tail_new[:qkv_cols].T,
            tail_new[qkv_cols : qkv_cols + out_cols].T,
            up_new.T,
            down_new.T,
        ]
        grad_vec = tail_new[qkv_cols + out_cols :].reshape(-1)[:vec_len]
        moments = [
            muon_keep * old + grad
            for old, grad in zip([qkv_moment, out_moment, up_moment, down_moment], grads)
        ]
        most = max(m.shape[1] for m in moments)
        padded = [jnp.pad(m, ((0, 0), (0, most - m.shape[1]))) for m in moments]
        chosen = padded[-1]
        for index in range(len(padded) - 2, -1, -1):
            chosen = jnp.where(head_id == index, padded[index], chosen)
        gram_mat = lax.dot_general(
            chosen, chosen, (((1,), (1,)), ((), ())), precision=lax.Precision.HIGH
        )
        own_factor = orthogonalize(lax.psum(gram_mat, "dp"), chosen)
        across = swap(own_factor, "head", 2)
        low_pair = jnp.where(side == 0, own_factor, across)
        high_pair = jnp.where(side == 0, across, own_factor)
        near_low = swap(low_pair, "head", 1)
        near_high = swap(high_pair, "head", 1)
        factors = [
            jnp.where(core == 0, low_pair, near_low),
            jnp.where(core == 0, near_low, low_pair),
            jnp.where(core == 0, high_pair, near_high),
            jnp.where(core == 0, near_high, high_pair),
        ]
        factors = [o[:, : m.shape[1]].astype(f32) for o, m in zip(factors, moments)]
        factors[3] = factors[3].T
        old_weights = [
            weight_block(qkv_weight, qkv_cols, 1),
            weight_block(out_weight, out_cols, 1),
            weight_block(up_weight, up_moment.shape[1], 1),
            weight_block(down_weight, down_moment.shape[1], 0),
        ]

        rates = (math.sqrt(3.0), 1.0, math.sqrt(max(1.0, hidden / width)), 1.0)
        new_weights = [
            old.astype(f32) * shrink - muon_rate * rate * factor
            for old, rate, factor in zip(old_weights, rates, factors)
        ]

    vec_old = lax.dynamic_slice_in_dim(vectors, dp_id * vec_len, vec_len, 0)
    vec_first = beta_first * adam_first + (1.0 - beta_first) * grad_vec
    vec_second = beta_second * adam_second + (1.0 - beta_second) * grad_vec * grad_vec
    first_hat = vec_first / (1.0 - beta_first**STEP)
    second_hat = vec_second / (1.0 - beta_second**STEP)
    vec_new = vec_old - adam_rate * first_hat / (jnp.sqrt(second_hat) + adam_eps)
    return (mixed, input_grad, *moments, *new_weights, vec_first, vec_second, vec_new)


def solution(mesh):
    tokens_spec = P(("dp", "head"), None)
    block_spec = P(None, "dp")
    return jax.shard_map(
        local,
        mesh=mesh,
        in_specs=(
            tokens_spec,
            tokens_spec,
            P(),
            P(),
            P(),
            P(),
            P(),
            block_spec,
            block_spec,
            block_spec,
            block_spec,
            P("dp"),
            P("dp"),
            P("dp"),
            P("dp", None),
        ),
        out_specs=(
            tokens_spec,
            tokens_spec,
            block_spec,
            block_spec,
            block_spec,
            block_spec,
            block_spec,
            block_spec,
            block_spec,
            P("dp", None),
            P("dp"),
            P("dp"),
            P("dp"),
        ),
        check_vma=False,
    )
```

profile of v0, /device:TPU:1, one launch (start us, length us, event | category | flops | bytes accessed | tf_op | source)
XLA Modules:
  0.0 187.8 jit_solution(17499621800769146875)
XLA Ops:
  1.3 106.2 %layer.1 = (f32[256,768]{1,0:T(8,128)}, f32[256,768]{1,0:T(8,128)}, bf16[3,2,2,192,384]{4,3,2,1,0:T(8,128)(2,1)}, f32[16,128]{1,0:T(8,128)}) custom-call(s32[1]{0:T(128)S(6)} %copy.28.row_class, s32[1,8]{1,0:T(1,128)} %lengths.1, bf16[256,768]{1,0:T(8,128)(2,1)} %tokens.1, bf16[256,768]{1,0:T(8,128)(2,1)} %cotangent.1, f32[1,9216]{1,0:T(1,128)} %bitcast.21, ...), custom_call_target="tpu_custom_call" | custom-call | tf_op jit(solution)/shard_map/layer/pallas_call | solution.py:864
  107.5 0.0 copy-start
  107.5 0.0 copy-start.1
  107.5 0.0 copy-start.2
  107.5 0.0 copy-start.3
  107.5 0.0 copy-start.4
  107.5 0.0 copy-start.5
  107.6 72.0 %muon_factors.1.factors_hbm = bf16[4,768,384]{2,1,0:T(8,128)(2,1)} custom-call(bf16[3,768,384]{2,1,0:T(8,128)(2,1)} %bitcast.19, f32[288,768]{1,0:T(8,128)} %bitcast.15, f32[96,768]{1,0:T(8,128)} %bitcast.17, f32[768,384]{1,0:T(8,128)} %up_old_hbm.1, f32[768,384]{1,0:T(8,128)} %down_old_hbm.1), custom_call_target="tpu_custom_call" | custom-call | tf_op jit(solution)/shard_map/muon_factors/pallas_call | solution.py:1150
  179.6 0.0 copy-done
  179.6 0.0 copy-done.1
  179.6 0.0 copy-done.2
  179.6 0.0 copy-done.3
  179.6 0.0 copy-done.4
  179.6 0.0 copy-done.5
  179.7 0.0 copy-start.6
  179.7 0.0 copy-start.7
  179.7 0.0 copy-start.8
  179.7 6.7 %finish.1 = (f32[256,768]{1,0:T(8,128)}, f32[256,768]{1,0:T(8,128)}, f32[288,768]{1,0:T(8,128)}, f32[96,768]{1,0:T(8,128)}, f32[768,384]{1,0:T(8,128)}, /*index=...) custom-call(bf16[4,768,384]{2,1,0:T(8,128)(2,1)} %muon_factors.1.factors_hb, ...), custom_call_target="tpu_custom_call" | custom-call | tf_op jit(solution)/shard_map/finish/pallas_call | solution.py:1310
  186.4 0.0 copy-done.6
  186.4 0.0 copy-done.7
  186.4 0.0 copy-done.8
  186.4 1.4 divide_subtract_fusion
Async XLA Ops:
  107.5 72.1 %copy-start = (f32[768,384]{1,0:T(8,128)S(1)}, f32[768,384]{1,0:T(8,128)}, u32[]{:S(2)}) copy-start(f32[768,384]{1,0:T(8,128)} %up_old_hbm.1) | copy-start | bytes 3538948
  107.5 72.1 %copy-start.1 = (bf16[768,768]{1,0:T(8,128)(2,1)S(1)}, bf16[768,768]{1,0:T(8,128)(2,1)}, u32[]{:S(2)}) copy-start(bf16[768,768]{1,0:T(8,128)(2,1)} %out_hbm.3) | copy-start | bytes 3538948
  107.5 72.1 %copy-start.2 = (f32[768,288]{0,1:T(8,128)S(1)}, f32[768,288]{0,1:T(8,128)}, u32[]{:S(2)}) copy-start(f32[768,288]{0,1:T(8,128)} %param.22) | copy-start | bytes 2654212
  107.5 72.1 %copy-start.3 = (f32[768,96]{0,1:T(8,128)S(1)}, f32[768,96]{0,1:T(8,128)}, u32[]{:S(2)}) copy-start(f32[768,96]{0,1:T(8,128)} %param.23) | copy-start | bytes 884740
  107.5 72.1 %copy-start.4 = (f32[256,768]{1,0:T(8,128)S(1)}, f32[256,768]{1,0:T(8,128)}, u32[]{:S(2)}) copy-start(f32[256,768]{1,0:T(8,128)} %get-tuple-element.28.mixed_hbm) | copy-start | bytes 2359300
  107.5 72.1 %copy-start.5 = (f32[256,768]{1,0:T(8,128)S(1)}, f32[256,768]{1,0:T(8,128)}, u32[]{:S(2)}) copy-start(f32[256,768]{1,0:T(8,128)} %get-tuple-element.29.grad_hbm) | copy-start | bytes 2359300
  179.7 6.7 %copy-start.6 = (f32[1152]{0:T(1024)S(1)}, f32[1152]{0:T(1024)}, u32[]{:S(2)}) copy-start(f32[1152]{0:T(1024)} %param.27) | copy-start | bytes 13828
  179.7 6.7 %copy-start.7 = (f32[1152]{0:T(1024)S(1)}, f32[1152]{0:T(1024)}, u32[]{:S(2)}) copy-start(f32[1152]{0:T(1024)} %param.26) | copy-start | bytes 13828
  179.7 6.7 %copy-start.8 = (f32[16,128]{1,0:T(8,128)S(1)}, f32[16,128]{1,0:T(8,128)}, u32[]{:S(2)}) copy-start(f32[16,128]{1,0:T(8,128)} %get-tuple-element.40) | copy-start | bytes 24580
where the time goes:
time: 188 us
  Pallas kernels  185 us (98%)
    pallas_call x1, Pallas kernels, layer(): pl.pallas_call(layer_kernel, out_shape=(jax.ShapeDtypeStruct((tok, D), f3...  106 us
    pallas_call x1, Pallas kernels, muon_factors(): pl.pallas_call(muon_kernel, out_shape=jax.ShapeDtypeStruct((4, size, cols...  72 us
    pallas_call x1, Pallas kernels, finish(): pl.pallas_call(finish_kernel, out_shape=tuple((jax.ShapeDtypeStruct(shape...  6.68 us

commit v1 on v0

--- a/solution.py
+++ b/solution.py
@@ -401,10 +401,13 @@
     out_hbm,
     up_hbm,
     down_hbm,
+    mixed_hbm,
+    grad_hbm,
+    sums_hbm,
+    vec_sum,
     mixed,
     input_grad,
     sums,
-    vec_sum,
     qkv_w,
     out_w,
     up_w,
@@ -446,6 +449,7 @@
     came_three,
     came_four,
     load_sem,
+    store_sem,
     pair_send,
     pair_recv,
     send_sem,
@@ -454,18 +458,28 @@
     grad_one = normed_one
     z, x, y, core = position()
     tok = tokens.shape[0]
+    thirds = [slice(index * D, (index + 1) * D) for index in range(3)]
     loads = {
         name: pltpu.make_async_copy(source, target, load_sem.at[index])
         for index, (name, source, target) in enumerate(
             (
-                ("qkv", qkv_hbm, qkv_w),
+                ("key", qkv_hbm.at[:, thirds[1]], qkv_w.at[:, thirds[1]]),
+                ("value", qkv_hbm.at[:, thirds[2]], qkv_w.at[:, thirds[2]]),
+                ("query", qkv_hbm.at[:, thirds[0]], qkv_w.at[:, thirds[0]]),
                 ("out", out_hbm, out_w),
                 ("up", up_hbm, up_w),
                 ("down", down_hbm, down_w),
             )
         )
     }
-    loads["qkv"].start()
+    for name in ("key", "value", "query"):
+        loads[name].start()
+    stores = []
+
+    def store(source, target):
+        stores.append(pltpu.make_async_copy(source, target, store_sem.at[len(stores)]))
+        stores[-1].start()
+
     beyond = device(z, x, 1 - y, core)
     beside = device(z, 1 - x, y, core)
     partner = device(z, x, y, 1 - core)
@@ -514,22 +528,23 @@
         narrow[own_rows, :] = value[:, own_half]
         return to_partner(value.at[:, other_half], narrow.at[far_rows])
 
-    loads["qkv"].wait()
-    for name in ("out", "up", "down"):
-        loads[name].start()
     kv_came = []
-    for index, start in ((1, None), (2, BIAS_VALUE)):
-        value = dot(tokens[...], qkv_w[:, index * D : (index + 1) * D], 1, 0)
+    for name, index, start in (("key", 1, None), ("value", 2, BIAS_VALUE)):
+        loads[name].wait()
+        value = dot(tokens[...], qkv_w[:, thirds[index]], 1, 0)
         if start is not None:
             value = value + span(start)
         cols = slice((index - 1) * D, index * D)
         keys_values[own_rows, cols] = value.astype(bf16)
         if index == 1:
             all_here()
+            for name in ("out", "up", "down"):
+                loads[name].start()
         kv_came.append(
             to_partner(keys_values.at[own_rows, cols], keys_values.at[far_rows, cols])
         )
-    value = dot(tokens[...], qkv_w[:, :D], 1, 0) + span(BIAS_QUERY)
+    loads["query"].wait()
+    value = dot(tokens[...], qkv_w[:, thirds[0]], 1, 0) + span(BIAS_QUERY)
     query[...] = value.astype(bf16)
     query_turned[...] = transposed(query[...])
     allowed = allowed_mask(row_class, lengths, 2 * y + core, tok)
@@ -614,6 +629,7 @@
 
     zero = jnp.zeros((8, D), f32)
     gain, shift, bias = by_rows(tok, norm_two, (zero, zero, zero))
+    store(mixed, mixed_hbm)
     put_vec(GAIN_TWO, column_sum(gain))
     put_vec(SHIFT_TWO, column_sum(shift))
     put_vec(BIAS_DOWN, column_sum(bias))
@@ -809,6 +825,7 @@
     vec_came = to_partner(vec, vec_core)
     value = dot(qkv_w[...], qkv_turned[:, own_lanes], 1, 0)
     input_grad[...] = grad_one[...] + value.T
+    store(input_grad, grad_hbm)
 
     vec_slots = [(send_sem.at[len(CHUNKS), i], recv_sem.at[len(CHUNKS), i]) for i in range(5)]
 
@@ -843,10 +860,18 @@
         yield
 
     steps = vec_steps()
+    left = [sum(chunk[0] == matrix for chunk in CHUNKS) for matrix in range(3)]
     for turn, index in enumerate(next(plan)):
         chains[index].advance()
+        matrix = CHUNKS[index][0]
+        left[matrix] -= chains[index].stage == 7
+        if not left[matrix]:
+            store(sums.at[matrix], sums_hbm.at[matrix])
+            left[matrix] = -1
         if turn % 10 == 9 and turn < 40:
             next(steps)
+    for copy in stores:
+        copy.wait()
     for copy in started:
         copy.wait_send()
 
@@ -870,8 +895,11 @@
             jax.ShapeDtypeStruct((16, LANES), f32),
         ),
         in_specs=[SMEM, SMEM, VMEM, VMEM, VMEM] + [ANY] * 4,
-        out_specs=(VMEM,) * 4,
+        out_specs=(ANY, ANY, ANY, VMEM),
         scratch_shapes=[
+            wide(tok, D),
+            wide(tok, D),
+            low(3, 2, 2, *side),
             low(D, 3 * D),
             low(D, D),
             low(D, FF),
@@ -912,7 +940,8 @@
             low(3, 2, 2, *side),
             low(3, 2, *side),
             low(3, *side),
-            pltpu.SemaphoreType.DMA((4,)),
+            pltpu.SemaphoreType.DMA((6,)),
+            pltpu.SemaphoreType.DMA((5,)),
             pltpu.SemaphoreType.DMA((12,)),
             pltpu.SemaphoreType.DMA((12,)),
             pltpu.SemaphoreType.DMA((len(CHUNKS) + 1, 6)),
@@ -1259,8 +1288,10 @@
     store(mixed_hbm, mixed_out)
     store(grad_hbm, grad_out)
 
-    def step(index, rate):
-        return muon_rate * rate * factors[index].astype(f32)
+    def step(index, rate, turned=False):
+        value = factors[index]
+        value = transposed(value) if turned else value
+        return muon_rate * rate * value.astype(f32)
 
     loads["sums"].wait()
     for index, name, target, out in (
@@ -1284,17 +1315,17 @@
     up_new[...] = up_w[...].astype(f32) * shrink - step(2, math.sqrt(max(1.0, FF / D)))
     store(up_new, up_out)
     loads["down"].wait()
-    down_new[...] = down_w[...].astype(f32) * shrink - step(3, 1.0).T
+    down_new[...] = down_w[...].astype(f32) * shrink - step(3, 1.0, True)
     store(down_new, down_out)
     loads["qkv"].wait()
-    turned[...] = qkv_w[...].astype(f32).T
+    turned[...] = transposed(qkv_w[...]).astype(f32)
     rows = pl.ds(pl.multiple_of(qkv_skip, 32), qkv_cols)
-    qkv_new[...] = turned[rows, :] * shrink - step(0, math.sqrt(3.0)).T[:qkv_cols]
+    qkv_new[...] = turned[rows, :] * shrink - step(0, math.sqrt(3.0), True)[:qkv_cols]
     store(qkv_new, qkv_out)
     loads["out"].wait()
-    turned[: out_w.shape[1], :] = out_w[...].astype(f32).T
+    turned[: out_w.shape[1], :] = transposed(out_w[...]).astype(f32)
     rows = pl.ds(pl.multiple_of(out_skip, 32), out_cols)
-    out_new[...] = turned[rows, :] * shrink - step(1, 1.0).T[qkv_cols:]
+    out_new[...] = turned[rows, :] * shrink - step(1, 1.0, True)[qkv_cols:]
     store(out_new, out_out)
     for copy in stores:
         copy.wait()

time: 188 us -> 187 us (level)
  no operation moved by 1% of the time
where the time goes in v1:
time: 187 us
  Pallas kernels  184 us (98%)
    pallas_call x1, Pallas kernels, layer(): pl.pallas_call(layer_kernel, out_shape=(jax.ShapeDtypeStruct((tok, D), f3...  105 us
    pallas_call x1, Pallas kernels, muon_factors(): pl.pallas_call(muon_kernel, out_shape=jax.ShapeDtypeStruct((4, size, cols...  72.6 us
    pallas_call x1, Pallas kernels, finish(): pl.pallas_call(finish_kernel, out_shape=tuple((jax.ShapeDtypeStruct(shape...  6.91 us

profile of v1, /device:TPU:1, one launch (start us, length us, event | category | flops | bytes accessed | tf_op | source)
XLA Modules:
  0.0 187.1 jit_solution(4899939563894737729)
XLA Ops:
  1.3 104.7 %layer.1 = (f32[256,768]{1,0:T(8,128)}, f32[256,768]{1,0:T(8,128)}, bf16[3,2,2,192,384]{4,3,2,1,0:T(8,128)(2,1)}, f32[16,128]{1,0:T(8,128)}) custom-call(s32[1]{0:T(128)S(6)} %copy.28.row_class, s32[1,8]{1,0:T(1,128)} %lengths.1, bf16[256,768]{1,0:T(8,128)(2,1)} %tokens.1, bf16[256,768]{1,0:T(8,128)(2,1)} %cotangent.1, f32[1,9216]{1,0:T(1,128)} %bitcast.21, ...), custom_call_target="tpu_custom_call" | custom-call | tf_op jit(solution)/shard_map/layer/pallas_call | solution.py:889
  106.0 0.0 copy-start
  106.0 0.0 copy-start.1
  106.0 0.0 copy-start.2
  106.0 0.0 copy-start.3
  106.0 0.0 copy-start.4
  106.1 0.0 copy-start.5
  106.1 72.6 %muon_factors.1.factors_hbm = bf16[4,768,384]{2,1,0:T(8,128)(2,1)} custom-call(bf16[3,768,384]{2,1,0:T(8,128)(2,1)} %bitcast.19, f32[288,768]{1,0:T(8,128)} %bitcast.15, f32[96,768]{1,0:T(8,128)} %bitcast.17, f32[768,384]{1,0:T(8,128)} %up_old_hbm.1, f32[768,384]{1,0:T(8,128)} %down_old_hbm.1), custom_call_target="tpu_custom_call" | custom-call | tf_op jit(solution)/shard_map/muon_factors/pallas_call | solution.py:1179
  178.7 0.0 copy-done
  178.7 0.0 copy-done.1
  178.7 0.0 copy-done.2
  178.7 0.0 copy-done.3
  178.7 0.0 copy-done.4
  178.8 0.0 copy-done.5
  178.8 0.0 copy-start.6
  178.8 0.0 copy-start.7
  178.8 0.0 copy-start.8
  178.8 6.9 %finish.1 = (f32[256,768]{1,0:T(8,128)}, f32[256,768]{1,0:T(8,128)}, f32[288,768]{1,0:T(8,128)}, f32[96,768]{1,0:T(8,128)}, f32[768,384]{1,0:T(8,128)}, /*index=...) custom-call(bf16[4,768,384]{2,1,0:T(8,128)(2,1)} %muon_factors.1.factors_hb, ...), custom_call_target="tpu_custom_call" | custom-call | tf_op jit(solution)/shard_map/finish/pallas_call | solution.py:1341
  185.7 0.0 copy-done.6
  185.7 0.0 copy-done.7
  185.7 0.0 copy-done.8
  185.8 1.4 divide_subtract_fusion
Async XLA Ops:
  106.0 72.7 %copy-start = (f32[768,384]{1,0:T(8,128)S(1)}, f32[768,384]{1,0:T(8,128)}, u32[]{:S(2)}) copy-start(f32[768,384]{1,0:T(8,128)} %up_old_hbm.1) | copy-start | bytes 3538948
  106.0 72.7 %copy-start.1 = (bf16[768,768]{1,0:T(8,128)(2,1)S(1)}, bf16[768,768]{1,0:T(8,128)(2,1)}, u32[]{:S(2)}) copy-start(bf16[768,768]{1,0:T(8,128)(2,1)} %out_hbm.3) | copy-start | bytes 3538948
  106.0 72.7 %copy-start.2 = (f32[768,288]{0,1:T(8,128)S(1)}, f32[768,288]{0,1:T(8,128)}, u32[]{:S(2)}) copy-start(f32[768,288]{0,1:T(8,128)} %param.22) | copy-start | bytes 2654212
  106.0 72.7 %copy-start.3 = (f32[768,96]{0,1:T(8,128)S(1)}, f32[768,96]{0,1:T(8,128)}, u32[]{:S(2)}) copy-start(f32[768,96]{0,1:T(8,128)} %param.23) | copy-start | bytes 884740
  106.0 72.7 %copy-start.4 = (f32[256,768]{1,0:T(8,128)S(1)}, f32[256,768]{1,0:T(8,128)}, u32[]{:S(2)}) copy-start(f32[256,768]{1,0:T(8,128)} %get-tuple-element.28.mixed_hbm) | copy-start | bytes 2359300
  106.1 72.7 %copy-start.5 = (f32[256,768]{1,0:T(8,128)S(1)}, f32[256,768]{1,0:T(8,128)}, u32[]{:S(2)}) copy-start(f32[256,768]{1,0:T(8,128)} %get-tuple-element.29.grad_hbm) | copy-start | bytes 2359300
  178.8 7.0 %copy-start.6 = (f32[1152]{0:T(1024)S(1)}, f32[1152]{0:T(1024)}, u32[]{:S(2)}) copy-start(f32[1152]{0:T(1024)} %param.27) | copy-start | bytes 13828
  178.8 7.0 %copy-start.7 = (f32[1152]{0:T(1024)S(1)}, f32[1152]{0:T(1024)}, u32[]{:S(2)}) copy-start(f32[1152]{0:T(1024)} %param.26) | copy-start | bytes 13828
  178.8 7.0 %copy-start.8 = (f32[16,128]{1,0:T(8,128)S(1)}, f32[16,128]{1,0:T(8,128)}, u32[]{:S(2)}) copy-start(f32[16,128]{1,0:T(8,128)} %get-tuple-element.40) | copy-start | bytes 24580

commit v2 on v1

--- a/solution.py
+++ b/solution.py
@@ -981,6 +981,7 @@
     out_hbm,
     up_hbm,
     down_hbm,
+    factors_hbm,
     factors,
     own_sum,
     qkv_old,
@@ -1058,18 +1059,21 @@
     low[...] = (moment[...] - high[...].astype(f32)).astype(bf16)
     started = []
 
-    def product(index):
-        i, j = blocks[index]
-        left, right = pl.ds(i * SUB, SUB), pl.ds(j * SUB, SUB)
+    def products(first, count):
+        i, j = blocks[first]
+        count = min(count, sum(row == i for row, _ in blocks[first:]))
+        left, right = pl.ds(i * SUB, SUB), pl.ds(j * SUB, count * SUB)
         total = dot(high[left, :], high[right, :], 1, 1)
         total = total + dot(high[left, :], low[right, :], 1, 1)
         total = total + dot(low[left, :], high[right, :], 1, 1)
         rows = SUB // 8
-        for owner in range(8):
-            cell = (owner // 4, owner // 2 % 2, owner % 2)
-            part[cell + (index,)] = total[
-                owner * rows : (owner + 1) * rows
-            ]
+        for index in range(count):
+            for owner in range(8):
+                cell = (owner // 4, owner // 2 % 2, owner % 2, first + index)
+                part[cell] = total[
+                    owner * rows : (owner + 1) * rows, index * SUB : (index + 1) * SUB
+                ]
+        return count
 
     def send(source, target, group, slot, axis):
         copy = pltpu.make_async_remote_copy(
@@ -1124,8 +1128,9 @@
     walks = [Walk(group) for group in range(len(GRAM_GROUPS))]
     for group in GRAM_PLAN:
         if walks[group].stage == 0:
-            for index in range(starts[group], starts[group] + GRAM_GROUPS[group][0]):
-                product(index)
+            first, end = starts[group], starts[group] + GRAM_GROUPS[group][0]
+            while first < end:
+                first += products(first, end - first)
         walks[group].advance()
 
     e = ortho[0]
@@ -1158,11 +1163,30 @@
         beside.append(share(own, rows, 1, partner))
 
     newton_schulz(e, moment, *ortho, emit)
+    far = 2 * (1 - y) + core
+    stores = []
+
+    def store(slot):
+        copy = pltpu.make_async_copy(
+            factors.at[slot], factors_hbm.at[slot], load_sem.at[2 + len(stores)]
+        )
+        copy.start()
+        stores.append(copy)
+
+    store(own)
+    for copy in beside:
+        copy.wait_recv()
+    store(2 * y + 1 - core)
+    passed = []
     for rows, copy in across:
         copy.wait_recv()
-        beside.append(share(2 * (1 - y) + core, rows, 2, partner))
-    for copy in beside:
+        passed.append(share(far, rows, 2, partner))
+    store(far)
+    for copy in passed:
         copy.wait_recv()
+    store(2 * (1 - y) + 1 - core)
+    for copy in stores:
+        copy.wait()
     for copy in started:
         copy.wait_send()
 
@@ -1180,8 +1204,9 @@
         muon_kernel,
         out_shape=jax.ShapeDtypeStruct((4, size, cols), bf16),
         in_specs=[ANY] * 5,
-        out_specs=VMEM,
+        out_specs=ANY,
         scratch_shapes=[
+            pltpu.VMEM((4, size, cols), bf16),
             pltpu.VMEM((size, cols), bf16),
             wide(*olds[0].shape),
             wide(*olds[1].shape),
@@ -1194,7 +1219,7 @@
             wide(count, *rows),
             pltpu.VMEM((size, cols), bf16),
             pltpu.VMEM((size, cols), bf16),
-            pltpu.SemaphoreType.DMA((2,)),
+            pltpu.SemaphoreType.DMA((6,)),
             pltpu.SemaphoreType.DMA((groups, 6)),
             pltpu.SemaphoreType.DMA((groups, 6)),
             pltpu.SemaphoreType.DMA((size // TILE, 3)),
@@ -1227,6 +1252,10 @@
     down_old_hbm,
     mixed_hbm,
     grad_hbm,
+    vec_grad,
+    vectors,
+    first_old,
+    second_old,
     mixed_out,
     grad_out,
     qkv_moment_out,
@@ -1237,6 +1266,9 @@
     out_out,
     up_out,
     down_out,
+    first_new,
+    second_new,
+    vec_new,
     factors,
     sums,
     qkv_w,
@@ -1288,6 +1320,19 @@
     store(mixed_hbm, mixed_out)
     store(grad_hbm, grad_out)
 
+    grad = vec_grad[:VEC_BLOCK]
+    first = beta_first * first_old[...] + (1.0 - beta_first) * grad
+    second = beta_second * second_old[...] + (1.0 - beta_second) * grad * grad
+    first_new[...] = first
+    second_new[...] = second
+    first = first / (1.0 - beta_first**STEP)
+    second = second / (1.0 - beta_second**STEP)
+    own = jnp.zeros_like(grad)
+    for index in range(8):
+        rows = vectors[index * VEC_BLOCK : (index + 1) * VEC_BLOCK]
+        own = jnp.where(dp_id == index, rows, own)
+    vec_new[...] = own - adam_rate * first / (jnp.sqrt(second) + adam_eps)
+
     def step(index, rate, turned=False):
         value = factors[index]
         value = transposed(value) if turned else value
@@ -1331,7 +1376,7 @@
         copy.wait()
 
 
-def finish(factors, sums, weights, olds, mixed, input_grad):
+def finish(factors, sums, weights, olds, mixed, input_grad, vec, vectors, adam):
     shapes = [old.shape for old in olds]
     news = shapes[:3] + [shapes[3][::-1]]
 
@@ -1342,10 +1387,10 @@
         finish_kernel,
         out_shape=tuple(
             jax.ShapeDtypeStruct(shape, f32)
-            for shape in [mixed.shape, input_grad.shape] + shapes + news
+            for shape in [mixed.shape, input_grad.shape] + shapes + news + [(VEC_BLOCK, LANES)] * 3
         ),
-        in_specs=[ANY] * 12,
-        out_specs=(ANY,) * 10,
+        in_specs=[ANY] * 12 + [VMEM] * 4,
+        out_specs=(ANY,) * 10 + (VMEM,) * 3,
         scratch_shapes=[
             pltpu.VMEM(factors.shape, bf16),
             pltpu.VMEM(sums.shape, bf16),
@@ -1362,7 +1407,7 @@
         ],
         compiler_params=pltpu.CompilerParams(vmem_limit_bytes=48 * MIB),
         name="finish",
-    )(factors, sums, *weights, *olds, mixed, input_grad)
+    )(factors, sums, *weights, *olds, mixed, input_grad, vec, vectors, *adam)
 
 
 def swap(value, axis, bit):
@@ -1438,7 +1483,6 @@
             up_weight,
             down_weight,
         )
-        grad_vec = vec[:VEC_BLOCK].reshape(vec_len)
         sums = sums.reshape(3, width, -1)
         olds = [qkv_moment.T, out_moment.T, up_moment, down_moment]
         mixed, input_grad, *results = finish(
@@ -1448,8 +1492,12 @@
             olds,
             mixed,
             input_grad,
+            vec,
+            vectors.reshape(-1, LANES),
+            [adam_first.reshape(-1, LANES), adam_second.reshape(-1, LANES)],
         )
-        moments, new_weights = results[:4], results[4:]
+        moments, new_weights = results[:4], results[4:8]
+        vec_first, vec_second, vec_new = (value.reshape(vec_len) for value in results[8:])
         moments = [moments[0].T, moments[1].T, *moments[2:]]
         new_weights = [new_weights[0].T, new_weights[1].T, *new_weights[2:]]
     else:
@@ -1611,12 +1659,12 @@
             for old, rate, factor in zip(old_weights, rates, factors)
         ]
 
-    vec_old = lax.dynamic_slice_in_dim(vectors, dp_id * vec_len, vec_len, 0)
-    vec_first = beta_first * adam_first + (1.0 - beta_first) * grad_vec
-    vec_second = beta_second * adam_second + (1.0 - beta_second) * grad_vec * grad_vec
-    first_hat = vec_first / (1.0 - beta_first**STEP)
-    second_hat = vec_second / (1.0 - beta_second**STEP)
-    vec_new = vec_old - adam_rate * first_hat / (jnp.sqrt(second_hat) + adam_eps)
+        vec_old = lax.dynamic_slice_in_dim(vectors, dp_id * vec_len, vec_len, 0)
+        vec_first = beta_first * adam_first + (1.0 - beta_first) * grad_vec
+        vec_second = beta_second * adam_second + (1.0 - beta_second) * grad_vec * grad_vec
+        first_hat = vec_first / (1.0 - beta_first**STEP)
+        second_hat = vec_second / (1.0 - beta_second**STEP)
+        vec_new = vec_old - adam_rate * first_hat / (jnp.sqrt(second_hat) + adam_eps)
     return (mixed, input_grad, *moments, *new_weights, vec_first, vec_second, vec_new)
 
 

time: 187 us -> 186 us (level)
  no operation moved by 1% of the time
where the time goes in v2:
time: 186 us
  Pallas kernels  184 us (99%)
    pallas_call x1, Pallas kernels, layer(): pl.pallas_call(layer_kernel, out_shape=(jax.ShapeDtypeStruct((tok, D), f3...  105 us
    pallas_call x1, Pallas kernels, muon_factors(): pl.pallas_call(muon_kernel, out_shape=jax.ShapeDtypeStruct((4, size, cols...  71.9 us
    pallas_call x1, Pallas kernels, finish(): pl.pallas_call(finish_kernel, out_shape=tuple((jax.ShapeDtypeStruct(shape...  7.54 us

profile of v2, /device:TPU:1, one launch (start us, length us, event | category | flops | bytes accessed | tf_op | source)
XLA Modules:
  0.0 185.8 jit_solution(12459978021539745894)
XLA Ops:
  1.3 104.7 %layer.1 = (f32[256,768]{1,0:T(8,128)}, f32[256,768]{1,0:T(8,128)}, bf16[3,2,2,192,384]{4,3,2,1,0:T(8,128)(2,1)}, f32[16,128]{1,0:T(8,128)}) custom-call(s32[1]{0:T(128)S(6)} %copy.28.row_class, s32[1,8]{1,0:T(1,128)} %lengths.1, bf16[256,768]{1,0:T(8,128)(2,1)} %tokens.1, bf16[256,768]{1,0:T(8,128)(2,1)} %cotangent.1, f32[1,9216]{1,0:T(1,128)} %bitcast.18, ...), custom_call_target="tpu_custom_call" | custom-call | tf_op jit(solution)/shard_map/layer/pallas_call | solution.py:889
  106.0 0.0 copy-start
  106.0 0.0 copy-start.1
  106.0 0.0 copy-start.2
  106.0 0.0 copy-start.3
  106.0 0.0 copy-start.4
  106.1 0.0 copy-start.5
  106.1 0.0 copy-start.6
  106.1 0.0 copy-start.7
  106.1 0.0 copy-start.8
  106.1 0.0 copy-start.9
  106.1 71.9 %muon_factors.1.factors_hbm = bf16[4,768,384]{2,1,0:T(8,128)(2,1)} custom-call(bf16[3,768,384]{2,1,0:T(8,128)(2,1)} %bitcast.22, f32[288,768]{1,0:T(8,128)} %bitcast.14, f32[96,768]{1,0:T(8,128)} %bitcast.16, f32[768,384]{1,0:T(8,128)} %up_old_hbm.1, f32[768,384]{1,0:T(8,128)} %down_old_hbm.1), custom_call_target="tpu_custom_call" | custom-call | tf_op jit(solution)/shard_map/muon_factors/pallas_call | solution.py:1203
  178.0 0.0 copy-done
  178.0 0.0 copy-done.1
  178.0 0.0 copy-done.2
  178.0 0.0 copy-done.3
  178.0 0.0 copy-done.4
  178.0 0.0 copy-done.5
  178.0 0.0 copy-done.6
  178.1 0.0 copy-done.7
  178.1 0.0 copy-done.8
  178.1 0.0 copy-done.9
  178.1 7.5 %finish.1 = (f32[256,768]{1,0:T(8,128)}, f32[256,768]{1,0:T(8,128)}, f32[288,768]{1,0:T(8,128)}, f32[96,768]{1,0:T(8,128)}, f32[768,384]{1,0:T(8,128)}, /*index=...) custom-call(bf16[4,768,384]{2,1,0:T(8,128)(2,1)} %muon_factors.1.fac, ...), custom_call_target="tpu_custom_call" | custom-call | tf_op jit(solution)/shard_map/finish/pallas_call | solution.py:1386
Async XLA Ops:
  106.0 72.0 %copy-start = (f32[768,384]{1,0:T(8,128)S(1)}, f32[768,384]{1,0:T(8,128)}, u32[]{:S(2)}) copy-start(f32[768,384]{1,0:T(8,128)} %up_old_hbm.1) | copy-start | bytes 3538948
  106.0 72.0 %copy-start.1 = (bf16[768,768]{1,0:T(8,128)(2,1)S(1)}, bf16[768,768]{1,0:T(8,128)(2,1)}, u32[]{:S(2)}) copy-start(bf16[768,768]{1,0:T(8,128)(2,1)} %out_hbm.3) | copy-start | bytes 3538948
  106.0 72.0 %copy-start.2 = (f32[768,288]{0,1:T(8,128)S(1)}, f32[768,288]{0,1:T(8,128)}, u32[]{:S(2)}) copy-start(f32[768,288]{0,1:T(8,128)} %param.22) | copy-start | bytes 2654212
  106.0 72.0 %copy-start.3 = (f32[768,96]{0,1:T(8,128)S(1)}, f32[768,96]{0,1:T(8,128)}, u32[]{:S(2)}) copy-start(f32[768,96]{0,1:T(8,128)} %param.23) | copy-start | bytes 884740
  106.0 72.0 %copy-start.4 = (f32[256,768]{1,0:T(8,128)S(1)}, f32[256,768]{1,0:T(8,128)}, u32[]{:S(2)}) copy-start(f32[256,768]{1,0:T(8,128)} %get-tuple-element.31.mixed_hbm) | copy-start | bytes 2359300
  106.1 72.0 %copy-start.5 = (f32[256,768]{1,0:T(8,128)S(1)}, f32[256,768]{1,0:T(8,128)}, u32[]{:S(2)}) copy-start(f32[256,768]{1,0:T(8,128)} %get-tuple-element.32.grad_hbm) | copy-start | bytes 2359300
  106.1 72.0 %copy-start.6 = (f32[9216]{0:T(1024)S(1)}, f32[9216]{0:T(1024)}, u32[]{:S(2)}) copy-start(f32[9216]{0:T(1024)} %param.21) | copy-start | bytes 110596
  106.1 72.0 %copy-start.7 = (f32[1152]{0:T(1024)S(1)}, f32[1152]{0:T(1024)}, u32[]{:S(2)}) copy-start(f32[1152]{0:T(1024)} %param.26) | copy-start | bytes 13828
  106.1 72.0 %copy-start.8 = (f32[1152]{0:T(1024)S(1)}, f32[1152]{0:T(1024)}, u32[]{:S(2)}) copy-start(f32[1152]{0:T(1024)} %param.27) | copy-start | bytes 13828
  106.1 72.0 %copy-start.9 = (f32[16,128]{1,0:T(8,128)S(1)}, f32[16,128]{1,0:T(8,128)}, u32[]{:S(2)}) copy-start(f32[16,128]{1,0:T(8,128)} %get-tuple-element.33.vec_grad) | copy-start | bytes 24580

commit v3 on v2

--- a/solution.py
+++ b/solution.py
@@ -364,19 +364,6 @@
 
 def column_sum(value):
     return jnp.sum(value, axis=0, keepdims=True)
-
-
-def normal_parts(value):
-    size = jnp.abs(value)
-    decay = jnp.exp(-0.5 * value * value)
-    below = 1.0 + (0.3275911 * 0.5**0.5) * size
-    t = pl.reciprocal(below, approx=True)
-    t = t * (2.0 - below * t)
-    series = t * (1.061405429 * 0.5)
-    for term in (-1.453152027, 1.421413741, -0.284496736, 0.254829592):
-        series = (series + term * 0.5) * t
-    tail = series * decay
-    return jnp.where(value < 0.0, tail, 1.0 - tail), decay * (1.0 / math.sqrt(2.0 * math.pi))
 
 
 def transposed(value):
@@ -602,7 +589,8 @@
 
         def gelu(rows, carry):
             value = work[rows, :] + span(BIAS_UP + cols.start)
-            chance, density = normal_parts(value)
+            chance = 0.5 * (1.0 + lax.erf(value * (0.5**0.5)))
+            density = jnp.exp(-0.5 * value * value) * (1.0 / math.sqrt(2.0 * math.pi))
             active[rows, cols] = (value * chance).astype(bf16)
             slope[rows, cols] = chance + value * density
             return carry

time: 186 us -> 184 us (0.989)
  Pallas kernels: 184 us -> 182 us
where the time goes in v3:
time: 184 us; the launch traced here: 183 us
  Pallas kernels  182 us (99%)
    pallas_call x1, Pallas kernels, layer(): pl.pallas_call(layer_kernel, out_shape=(jax.ShapeDtypeStruct((tok, D), f3...  103 us
    pallas_call x1, Pallas kernels, muon_factors(): pl.pallas_call(muon_kernel, out_shape=jax.ShapeDtypeStruct((4, size, cols...  71.2 us
    pallas_call x1, Pallas kernels, finish(): pl.pallas_call(finish_kernel, out_shape=tuple((jax.ShapeDtypeStruct(shape...  7.54 us

profile of v3, /device:TPU:1, one launch (start us, length us, event | category | flops | bytes accessed | tf_op | source)
XLA Modules:
  0.0 183.3 jit_solution(5605095636606314782)
XLA Ops:
  1.3 102.9 %layer.1 = (f32[256,768]{1,0:T(8,128)}, f32[256,768]{1,0:T(8,128)}, bf16[3,2,2,192,384]{4,3,2,1,0:T(8,128)(2,1)}, f32[16,128]{1,0:T(8,128)}) custom-call(s32[1]{0:T(128)S(6)} %copy.28.row_class, s32[1,8]{1,0:T(1,128)} %lengths.1, bf16[256,768]{1,0:T(8,128)(2,1)} %tokens.1, bf16[256,768]{1,0:T(8,128)(2,1)} %cotangent.1, f32[1,9216]{1,0:T(1,128)} %bitcast.18, ...), custom_call_target="tpu_custom_call" | custom-call | tf_op jit(solution)/shard_map/layer/pallas_call | solution.py:877
  104.2 0.0 copy-start
  104.2 0.0 copy-start.1
  104.2 0.0 copy-start.2
  104.2 0.0 copy-start.3
  104.2 0.0 copy-start.4
  104.2 0.0 copy-start.5
  104.2 0.0 copy-start.6
  104.2 0.0 copy-start.7
  104.3 0.0 copy-start.8
  104.3 0.0 copy-start.9
  104.3 71.2 %muon_factors.1.factors_hbm = bf16[4,768,384]{2,1,0:T(8,128)(2,1)} custom-call(bf16[3,768,384]{2,1,0:T(8,128)(2,1)} %bitcast.22, f32[288,768]{1,0:T(8,128)} %bitcast.14, f32[96,768]{1,0:T(8,128)} %bitcast.16, f32[768,384]{1,0:T(8,128)} %up_old_hbm.1, f32[768,384]{1,0:T(8,128)} %down_old_hbm.1), custom_call_target="tpu_custom_call" | custom-call | tf_op jit(solution)/shard_map/muon_factors/pallas_call | solution.py:1191
  175.5 0.0 copy-done
  175.5 0.0 copy-done.1
  175.5 0.0 copy-done.2
  175.5 0.0 copy-done.3
  175.6 0.0 copy-done.4
  175.6 0.0 copy-done.5
  175.6 0.0 copy-done.6
  175.6 0.0 copy-done.7
  175.6 0.0 copy-done.8
  175.6 0.0 copy-done.9
  175.6 7.5 %finish.1 = (f32[256,768]{1,0:T(8,128)}, f32[256,768]{1,0:T(8,128)}, f32[288,768]{1,0:T(8,128)}, f32[96,768]{1,0:T(8,128)}, f32[768,384]{1,0:T(8,128)}, /*index=...) custom-call(bf16[4,768,384]{2,1,0:T(8,128)(2,1)} %muon_factors.1.fac, ...), custom_call_target="tpu_custom_call" | custom-call | tf_op jit(solution)/shard_map/finish/pallas_call | solution.py:1374
Async XLA Ops:
  104.2 71.4 %copy-start = (f32[768,384]{1,0:T(8,128)S(1)}, f32[768,384]{1,0:T(8,128)}, u32[]{:S(2)}) copy-start(f32[768,384]{1,0:T(8,128)} %up_old_hbm.1) | copy-start | bytes 3538948
  104.2 71.4 %copy-start.1 = (bf16[768,768]{1,0:T(8,128)(2,1)S(1)}, bf16[768,768]{1,0:T(8,128)(2,1)}, u32[]{:S(2)}) copy-start(bf16[768,768]{1,0:T(8,128)(2,1)} %out_hbm.3) | copy-start | bytes 3538948
  104.2 71.4 %copy-start.2 = (f32[768,288]{0,1:T(8,128)S(1)}, f32[768,288]{0,1:T(8,128)}, u32[]{:S(2)}) copy-start(f32[768,288]{0,1:T(8,128)} %param.22) | copy-start | bytes 2654212
  104.2 71.4 %copy-start.3 = (f32[768,96]{0,1:T(8,128)S(1)}, f32[768,96]{0,1:T(8,128)}, u32[]{:S(2)}) copy-start(f32[768,96]{0,1:T(8,128)} %param.23) | copy-start | bytes 884740
  104.2 71.4 %copy-start.4 = (f32[256,768]{1,0:T(8,128)S(1)}, f32[256,768]{1,0:T(8,128)}, u32[]{:S(2)}) copy-start(f32[256,768]{1,0:T(8,128)} %get-tuple-element.31.mixed_hbm) | copy-start | bytes 2359300
  104.2 71.4 %copy-start.5 = (f32[256,768]{1,0:T(8,128)S(1)}, f32[256,768]{1,0:T(8,128)}, u32[]{:S(2)}) copy-start(f32[256,768]{1,0:T(8,128)} %get-tuple-element.32.grad_hbm) | copy-start | bytes 2359300
  104.2 71.4 %copy-start.6 = (f32[9216]{0:T(1024)S(1)}, f32[9216]{0:T(1024)}, u32[]{:S(2)}) copy-start(f32[9216]{0:T(1024)} %param.21) | copy-start | bytes 110596
  104.2 71.3 %copy-start.7 = (f32[1152]{0:T(1024)S(1)}, f32[1152]{0:T(1024)}, u32[]{:S(2)}) copy-start(f32[1152]{0:T(1024)} %param.26) | copy-start | bytes 13828
  104.3 71.3 %copy-start.8 = (f32[1152]{0:T(1024)S(1)}, f32[1152]{0:T(1024)}, u32[]{:S(2)}) copy-start(f32[1152]{0:T(1024)} %param.27) | copy-start | bytes 13828
  104.3 71.3 %copy-start.9 = (f32[16,128]{1,0:T(8,128)S(1)}, f32[16,128]{1,0:T(8,128)}, u32[]{:S(2)}) copy-start(f32[16,128]{1,0:T(8,128)} %get-tuple-element.33.vec_grad) | copy-start | bytes 24580

commit v4 on v3

--- a/solution.py
+++ b/solution.py
@@ -168,7 +168,7 @@
 
 
 CENTRES = (0.0, 0.0, 0.0, 0.8, 0.8)
-TILE = 256
+TILE = 384
 SUB = 128
 
 
@@ -535,6 +535,7 @@
     query[...] = value.astype(bf16)
     query_turned[...] = transposed(query[...])
     allowed = allowed_mask(row_class, lengths, 2 * y + core, tok)
+    penalty = jnp.where(allowed, 0.0, masked_score)
     masks, first = half_masks()
     tokens_came = share_half(tokens, narrow_tokens)
     for copy in kv_came:
@@ -551,8 +552,7 @@
         values = keys_values[:, lanes_at(D + pair * LANES)]
         outs = []
         for side, mask in enumerate(masks):
-            score = dot(query[:, cols] * (mask * scale), keys, 1, 1)
-            score = jnp.where(allowed, score, masked_score)
+            score = dot(query[:, cols] * (mask * scale), keys, 1, 1) + penalty
             exponent = jnp.exp(score - jnp.max(score, axis=-1, keepdims=True))
             chance = exponent * (1.0 / jnp.sum(exponent, axis=-1, keepdims=True))
             chance = chance.astype(bf16)

time: 184 us -> 184 us (level)
  no operation moved by 1% of the time
where the time goes in v4:
time: 184 us
  Pallas kernels  182 us (99%)
    pallas_call x1, Pallas kernels, layer(): pl.pallas_call(layer_kernel, out_shape=(jax.ShapeDtypeStruct((tok, D), f3...  103 us
    pallas_call x1, Pallas kernels, muon_factors(): pl.pallas_call(muon_kernel, out_shape=jax.ShapeDtypeStruct((4, size, cols...  71.7 us
    pallas_call x1, Pallas kernels, finish(): pl.pallas_call(finish_kernel, out_shape=tuple((jax.ShapeDtypeStruct(shape...  7.54 us

profile of v4, /device:TPU:1, one launch (start us, length us, event | category | flops | bytes accessed | tf_op | source)
XLA Modules:
  0.0 184.1 jit_solution(13337032598933986445)
XLA Ops:
  1.3 103.2 %layer.1 = (f32[256,768]{1,0:T(8,128)}, f32[256,768]{1,0:T(8,128)}, bf16[3,2,2,192,384]{4,3,2,1,0:T(8,128)(2,1)}, f32[16,128]{1,0:T(8,128)}) custom-call(s32[1]{0:T(128)S(6)} %copy.28.row_class, s32[1,8]{1,0:T(1,128)} %lengths.1, bf16[256,768]{1,0:T(8,128)(2,1)} %tokens.1, bf16[256,768]{1,0:T(8,128)(2,1)} %cotangent.1, f32[1,9216]{1,0:T(1,128)} %bitcast.18, ...), custom_call_target="tpu_custom_call" | custom-call | tf_op jit(solution)/shard_map/layer/pallas_call | solution.py:877
  104.5 0.0 copy-start
  104.5 0.0 copy-start.1
  104.6 0.0 copy-start.2
  104.6 0.0 copy-start.3
  104.6 0.0 copy-start.4
  104.6 0.0 copy-start.5
  104.6 0.0 copy-start.6
  104.6 0.0 copy-start.7
  104.6 0.0 copy-start.8
  104.6 0.0 copy-start.9
  104.6 71.7 %muon_factors.1.factors_hbm = bf16[4,768,384]{2,1,0:T(8,128)(2,1)} custom-call(bf16[3,768,384]{2,1,0:T(8,128)(2,1)} %bitcast.22, f32[288,768]{1,0:T(8,128)} %bitcast.14, f32[96,768]{1,0:T(8,128)} %bitcast.16, f32[768,384]{1,0:T(8,128)} %up_old_hbm.1, f32[768,384]{1,0:T(8,128)} %down_old_hbm.1), custom_call_target="tpu_custom_call" | custom-call | tf_op jit(solution)/shard_map/muon_factors/pallas_call | solution.py:1191
  176.3 0.0 copy-done
  176.3 0.0 copy-done.1
  176.3 0.0 copy-done.2
  176.3 0.0 copy-done.3
  176.3 0.0 copy-done.4
  176.4 0.0 copy-done.5
  176.4 0.0 copy-done.6
  176.4 0.0 copy-done.7
  176.4 0.0 copy-done.8
  176.4 0.0 copy-done.9
  176.4 7.5 %finish.1 = (f32[256,768]{1,0:T(8,128)}, f32[256,768]{1,0:T(8,128)}, f32[288,768]{1,0:T(8,128)}, f32[96,768]{1,0:T(8,128)}, f32[768,384]{1,0:T(8,128)}, /*index=...) custom-call(bf16[4,768,384]{2,1,0:T(8,128)(2,1)} %muon_factors.1.fac, ...), custom_call_target="tpu_custom_call" | custom-call | tf_op jit(solution)/shard_map/finish/pallas_call | solution.py:1374
Async XLA Ops:
  104.5 71.8 %copy-start = (f32[768,384]{1,0:T(8,128)S(1)}, f32[768,384]{1,0:T(8,128)}, u32[]{:S(2)}) copy-start(f32[768,384]{1,0:T(8,128)} %up_old_hbm.1) | copy-start | bytes 3538948
  104.5 71.8 %copy-start.1 = (bf16[768,768]{1,0:T(8,128)(2,1)S(1)}, bf16[768,768]{1,0:T(8,128)(2,1)}, u32[]{:S(2)}) copy-start(bf16[768,768]{1,0:T(8,128)(2,1)} %out_hbm.3) | copy-start | bytes 3538948
  104.6 71.8 %copy-start.2 = (f32[768,288]{0,1:T(8,128)S(1)}, f32[768,288]{0,1:T(8,128)}, u32[]{:S(2)}) copy-start(f32[768,288]{0,1:T(8,128)} %param.22) | copy-start | bytes 2654212
  104.6 71.8 %copy-start.3 = (f32[768,96]{0,1:T(8,128)S(1)}, f32[768,96]{0,1:T(8,128)}, u32[]{:S(2)}) copy-start(f32[768,96]{0,1:T(8,128)} %param.23) | copy-start | bytes 884740
  104.6 71.8 %copy-start.4 = (f32[256,768]{1,0:T(8,128)S(1)}, f32[256,768]{1,0:T(8,128)}, u32[]{:S(2)}) copy-start(f32[256,768]{1,0:T(8,128)} %get-tuple-element.31.mixed_hbm) | copy-start | bytes 2359300
  104.6 71.8 %copy-start.5 = (f32[256,768]{1,0:T(8,128)S(1)}, f32[256,768]{1,0:T(8,128)}, u32[]{:S(2)}) copy-start(f32[256,768]{1,0:T(8,128)} %get-tuple-element.32.grad_hbm) | copy-start | bytes 2359300
  104.6 71.8 %copy-start.6 = (f32[9216]{0:T(1024)S(1)}, f32[9216]{0:T(1024)}, u32[]{:S(2)}) copy-start(f32[9216]{0:T(1024)} %param.21) | copy-start | bytes 110596
  104.6 71.8 %copy-start.7 = (f32[1152]{0:T(1024)S(1)}, f32[1152]{0:T(1024)}, u32[]{:S(2)}) copy-start(f32[1152]{0:T(1024)} %param.26) | copy-start | bytes 13828
  104.6 71.8 %copy-start.8 = (f32[1152]{0:T(1024)S(1)}, f32[1152]{0:T(1024)}, u32[]{:S(2)}) copy-start(f32[1152]{0:T(1024)} %param.27) | copy-start | bytes 13828
  104.6 71.8 %copy-start.9 = (f32[16,128]{1,0:T(8,128)S(1)}, f32[16,128]{1,0:T(8,128)}, u32[]{:S(2)}) copy-start(f32[16,128]{1,0:T(8,128)} %get-tuple-element.33.vec_grad) | copy-start | bytes 24580
